TPU v7x, 256 devices: a whole 4x4x8 slice. The times are simulated.
256 devices in a mesh: lon: 16 (over y, x_hi, core), lat: 16 (over z, x_lo).
Axes of the slice: x: 4 (x_hi: 2, x_lo: 2; x = x_hi * 2 + x_lo), y: 4, z: 8, core: 2. Of those that a mesh axis runs over, the one named last changes fastest.
Arguments:
- potential_warmth: float32 [75, 128, 2048], P(None, 'lat', 'lon'), may hold values from -6 to 6
- saltiness_anomaly: float32 [75, 128, 2048], P(None, 'lat', 'lon'), may hold values from -6 to 6
- zonal_current: float32 [75, 128, 2048], P(None, 'lat', 'lon'), may hold values from -3 to 3
- meridional_current: float32 [75, 128, 2048], P(None, 'lat', 'lon'), may hold values from -3 to 3
- marine_indicator: int32 [75, 128, 2048], P(None, 'lat', 'lon'), may hold values 0 or 1
- bathymetry_layers: int32 [128, 2048], P('lat', 'lon'), may hold values from 1 to 75
- planetary_vorticity: float32 [128, 2048], P('lat', 'lon'), may hold values from -1.5 to 1.5
Outputs:
- temp_next: float32 [75, 128, 2048], P(None, 'lat', 'lon')
- salt_next: float32 [75, 128, 2048], P(None, 'lat', 'lon')
- east_next: float32 [75, 128, 2048], P(None, 'lat', 'lon')
- north_next: float32 [75, 128, 2048], P(None, 'lat', 'lon')
All inputs are finite; a program needn't handle non-finite values. No bound on the sum of `marine_indicator` on one device may be relied on, other than what follows from the above.
Results may differ from a plain program's by a relative error of at most 0.0003.
Values sent between devices are 32-bit elements; how exact they have to be, the bound alone decides.
No kernel may reach another device: no remote copies, remote signals or barrier semaphores. Data moves between devices by JAX's collectives and lax.ppermute only.
A program may use at most 128 MiB of HBM per device.

v0:
```python
import functools

import jax
import jax.numpy as jnp
from jax import lax
from jax.experimental import pallas as pl
from jax.experimental.pallas import tpu as pltpu
from jax.sharding import PartitionSpec as P

SIDE = 0.4
STEP = 0.1
THERMAL = 0.2
HALINE = 0.8
GRAVITY = 0.1
DRAG = 2.0
HIGH = lax.Precision.HIGHEST
UNROLL = 5


def levels_loop(levels, body, carry):
    unroll = UNROLL if levels % UNROLL == 0 else 1

    def group(index, carry):
        for step in range(unroll):
            carry = body(index * unroll + step, carry)
        return carry

    return lax.fori_loop(0, levels // unroll, group, carry)


def tile(k):
    return pl.ds(pl.multiple_of(8 * (k + 1), 8), 8)


def density(temp, salt):
    return HALINE * salt - THERMAL * temp


def tile_update(k, fields, above, below, around, wet, wet_v, wet_around, press, press_around, cor, bat):
    half_u, half_v = 0.5 * fields[2], 0.5 * fields[3]
    ways = (SIDE - half_u, SIDE + half_u, SIDE - half_v, SIDE + half_v)
    own = SIDE * wet_v
    for way, wet_n in zip(ways, wet_around):
        own = own + way * wet_n
    tend = []
    for f, up, down, sides in zip(fields, above, below, around):
        t = SIDE * (up + down) - own * f
        for way, q in zip(ways, sides):
            t = t + way * q
        tend.append(t)
    wet_e, wet_w, wet_n, wet_s = wet_around
    m_e, m_w, m_n, m_s = press_around
    gx = 0.5 * (m_e - m_w - press * (wet_e - wet_w))
    gy = 0.5 * (m_n - m_s - press * (wet_n - wet_s))
    rate = jnp.where(bat == k + 1, DRAG, 0.0)
    tend[2] = tend[2] + (cor * fields[3] - gx - rate * fields[2])
    tend[3] = tend[3] - (cor * fields[2] + gy + rate * fields[3])
    scale = STEP * wet
    return [f + scale * t for f, t in zip(fields, tend)]


def from_side(centre, other, way, to_u, to_v):
    scale = STEP * centre[4]
    wet_n = other[4]
    adds = [scale * (way * (other[i] - wet_n * centre[i])) for i in range(4)]
    push = (0.5 * scale) * (wet_n * (other[5] - centre[5]))
    if to_u:
        adds[2] = adds[2] + to_u * push
    if to_v:
        adds[3] = adds[3] + to_v * push
    return adds


def way_of(cell, side):
    if side == "east":
        return SIDE - 0.5 * cell[2]
    if side == "west":
        return SIDE + 0.5 * cell[2]
    if side == "north":
        return SIDE - 0.5 * cell[3]
    return SIDE + 0.5 * cell[3]


PUSH = {"east": (-1.0, 0.0), "west": (1.0, 0.0), "north": (0.0, -1.0), "south": (0.0, 1.0)}


def side_adds(cell, other, side):
    return from_side(cell, other, way_of(cell, side), *PUSH[side])


def iotas(shape=(8, 128)):
    return lax.broadcasted_iota(jnp.int32, shape, 0), lax.broadcasted_iota(jnp.int32, shape, 1)


def first_kernel(levels, place, temp, salt, east, north, sea, bat_ref, cor_ref,
                 part, wet_ref, xs, zb, on, off, state, press):
    lon_odd = place[0] % 2
    lat_odd = place[1] % 2
    sub, lane = iotas()
    bat, cor = bat_ref[...], cor_ref[...]
    zero = jnp.zeros((8, 128), jnp.float32)
    for i in range(4):
        for edge in (-1, levels):
            state[i, pl.ds(8 * (edge + 1), 8), :] = zero
    for edge in (-1, levels):
        wet_ref[pl.ds(8 * (edge + 1), 8), :] = zero

    def keep(k, columns, values):
        out = []
        here = lane == k
        for j, value in enumerate(values):
            out.append(jnp.where(here, pltpu.roll(value, k, 1), columns[2 * j]))
            out.append(jnp.where(here, pltpu.roll(value, k + 1, 1), columns[2 * j + 1]))
        return out

    def prepare(k, carry):
        total, columns = carry
        wet = jnp.where(k < bat, sea[k], 0).astype(jnp.float32)
        fields = [ref[k] * wet for ref in (temp, salt, east, north)]
        for i in range(4):
            state[i, tile(k), :] = fields[i]
        wet_ref[tile(k), :] = wet
        dens = density(fields[0], fields[1])
        total = total + dens
        p = GRAVITY * (total - 0.5 * dens)
        press[pl.ds(pl.multiple_of(8 * k, 8), 8), :] = p
        return total, keep(k, columns, fields + [wet, p])

    _, columns = levels_loop(levels, prepare, (zero, [zero] * 12))

    open_sides = (lane < 127, lane > 0, sub < 7, sub > 0)

    def beside(value):
        moved = (pltpu.roll(value, 127, 1), pltpu.roll(value, 1, 1), pltpu.roll(value, 7, 0), pltpu.roll(value, 1, 0))
        return [jnp.where(ok, m, 0.0) for ok, m in zip(open_sides, moved)]

    def partial(k, more):
        fields = [state[i, tile(k), :] for i in range(4)]
        above = [state[i, tile(k - 1), :] for i in range(4)]
        below = [state[i, tile(k + 1), :] for i in range(4)]
        wet = wet_ref[tile(k), :]
        wet_v = wet_ref[tile(k - 1), :] + wet_ref[tile(k + 1), :]
        p = press[pl.ds(pl.multiple_of(8 * k, 8), 8), :]
        new = tile_update(k, fields, above, below, [beside(f) for f in fields], wet, wet_v, beside(wet),
                          p, beside(wet * p), cor, bat)
        for i in range(4):
            part[i, tile(k), :] = new[i]
        return keep(k, more, new)

    more = levels_loop(levels, partial, [zero] * 8)
    for i in range(4):
        for edge in (-1, levels):
            part[i, pl.ds(8 * (edge + 1), 8), :] = zero

    for ref, row in ((xs, 7 - 7 * lat_odd), (zb, 7 * lat_odd)):
        rows = pl.ds(8 + row, levels, stride=8)
        planes = [state[i, rows, :] for i in range(4)] + [wet_ref[rows, :]] + [part[i, rows, :] for i in range(4)]
        for i, plane in enumerate(planes):
            ref[pl.ds(levels * i, levels), :] = plane
        left = ref.shape[0] - 9 * levels
        if left:
            ref[pl.ds(9 * levels, left), :] = jnp.zeros((left, 128), jnp.float32)
    columns = columns + more
    for j in range(10):
        west, eastern = columns[2 * j], columns[2 * j + 1]
        on[j] = jnp.where(lon_odd == 0, eastern, west)
        off[j] = jnp.where(lon_odd == 0, west, eastern)


def sides_of(lon_odd, on_own, off_own, on, off):
    odd = lon_odd == 1
    west = [jnp.where(odd, on_own[j], off_own[j]) for j in range(10)]
    east = [jnp.where(odd, off_own[j], on_own[j]) for j in range(10)]
    far_west = [jnp.where(odd, on[j], off[j]) for j in range(10)]
    far_east = [jnp.where(odd, off[j], on[j]) for j in range(10)]
    return west, east, far_west, far_east


def second_kernel(levels, place, part, on_own, off_own, on, off, full, corner_xs, corner_zb):
    lon_odd = place[0] % 2
    lat_odd = place[1] % 2
    sub, lane = iotas()
    west, east, far_west, far_east = sides_of(lon_odd, on_own, off_own, on, off)
    adds_w = side_adds(west[:6], far_west[:6], "west")
    adds_e = side_adds(east[:6], far_east[:6], "east")
    entries = far_west[:6] + adds_w + far_east[:6] + adds_e
    for ref, flag in ((corner_xs, lat_odd == 0), (corner_zb, lat_odd == 1)):
        for r, entry in enumerate(entries):
            ref[pl.ds(r, 1), :] = jnp.where(flag, entry[7:8, :], entry[0:1, :])
        ref[pl.ds(20, 4), :] = jnp.zeros((4, 128), jnp.float32)

    def add(k, carry):
        for i in range(4):
            extra_w = pltpu.roll(adds_w[i], 128 - k, 1)
            extra_e = pltpu.roll(adds_e[i], 127 - k, 1)
            extra = jnp.where(lane == 0, extra_w, jnp.where(lane == 127, extra_e, 0.0))
            full[i, tile(k), :] = part[i, tile(k), :] + extra
        return carry

    levels_loop(levels, add, 0)
    zero = jnp.zeros((8, 128), jnp.float32)
    for i in range(4):
        for edge in (-1, levels):
            full[i, pl.ds(8 * (edge + 1), 8), :] = zero


def third_kernel(levels, tops, place, full_in, wet_ref, bat_ref, cor_ref, xs_own, zb_own, xs, zb,
                 on_own, off_own, on, off, corner_xs, corner_zb,
                 temp, salt, east_out, north_out, full, halo, flipped):
    lon_odd = place[0] % 2
    lat_odd = place[1] % 2
    odd = lat_odd == 1
    top = place[1] == tops
    sub, lane = iotas()
    bat, cor = bat_ref[...], cor_ref[...]
    full[...] = full_in[...]

    south_c = jnp.where(odd, corner_xs[...], corner_zb[...])
    north_c = jnp.where(odd, corner_zb[...], corner_xs[...])
    r = lax.broadcasted_iota(jnp.int32, (24, 128), 0)
    swapped = jnp.concatenate([north_c[10:20], north_c[0:10], north_c[20:24]], axis=0)
    s = r % 10
    swapped = jnp.where((s == 2) | (s == 3) | (s == 8) | (s == 9), -swapped, swapped)
    north_c = jnp.where(top, swapped, north_c)

    west, east, far_west, far_east = sides_of(lon_odd, on_own, off_own, on, off)
    after = []
    for own, far, toward, base in ((west, far_west, "east", 0), (east, far_east, "west", 10)):
        new = list(far[6:10])
        south_cell = [south_c[base + i : base + i + 1, :] for i in range(6)]
        north_cell = [north_c[base + i : base + i + 1, :] for i in range(6)]
        for i, a in enumerate(side_adds(far[:6], own[:6], toward)):
            new[i] = new[i] + a
        for i, a in enumerate(side_adds(far[:6], south_cell, "south")):
            new[i] = new[i] + jnp.where(sub == 0, a, 0.0)
        for i, a in enumerate(side_adds(far[:6], north_cell, "north")):
            new[i] = new[i] + jnp.where(sub == 7, a, 0.0)
        after.append(new)
    row, col = iotas((128, 128))
    upper = jnp.where(row < col, 1.0, jnp.where(row == col, 0.5, 0.0))
    dens = jnp.concatenate([density(new[0], new[1]) for new in after], axis=0)
    p = GRAVITY * jnp.dot(dens, upper, precision=HIGH, preferred_element_type=jnp.float32)
    far_cols = []
    for j, (new, far) in enumerate(zip(after, (far_west, far_east))):
        far_cols.append(new + [far[4] * p[8 * j : 8 * j + 8], far[4]])

    @pl.when(jnp.logical_not(top))
    def _():
        flipped[...] = jnp.where(odd, zb[...], xs[...])

    @pl.when(top)
    def _():
        mirror = 127 - lax.broadcasted_iota(jnp.int32, (8, 128), 1)
        count = (9 * levels + 7) // 8

        def turn(t, carry):
            at = pl.ds(pl.multiple_of(8 * t, 8), 8)
            flipped[at, :] = jnp.take_along_axis(zb[at, :], mirror, axis=1, mode="promise_in_bounds")
            return carry

        lax.fori_loop(0, count, turn, 0)

    def plane(ref, i):
        return ref[pl.ds(levels * i, levels), :]

    sign = jnp.where(top, -1.0, 1.0)
    signs = [1.0, 1.0, sign, sign, 1.0, 1.0, 1.0, sign, sign]
    north_far = [plane(flipped, i) * signs[i] for i in range(9)]
    south_far = [jnp.where(odd, plane(xs, i), plane(zb, i)) for i in range(9)]
    north_own = [jnp.where(odd, plane(zb_own, i), plane(xs_own, i)) for i in range(5)]
    south_own = [jnp.where(odd, plane(xs_own, i), plane(zb_own, i)) for i in range(5)]
    row, col = iotas((levels, levels))
    lower = jnp.where(col < row, 1.0, jnp.where(row == col, 0.5, 0.0))

    def pressures(planes):
        dens = jnp.concatenate([density(f[0], f[1]) for f in planes], axis=1)
        p = GRAVITY * jnp.dot(lower, dens, precision=HIGH, preferred_element_type=jnp.float32)
        return [p[:, 128 * j : 128 * j + 128] for j in range(len(planes))]

    before = pressures([south_far, north_far, south_own, north_own])
    lanes = lax.broadcasted_iota(jnp.int32, (levels, 128), 1)
    corners = jnp.concatenate([south_c, north_c, jnp.zeros((80, 128), jnp.float32)], axis=0).T[:levels]
    results = []
    for n, (far, own, own_side, far_side, own_row) in enumerate(
        ((south_far, south_own, "south", "north", 0), (north_far, north_own, "north", "south", 7))
    ):
        far_cell = far[:5] + [before[n]]
        own_cell = own[:5] + [before[2 + n]]
        rows = pl.ds(8 + own_row, levels, stride=8)
        for i, a in enumerate(side_adds(own_cell, far_cell, own_side)):
            full[i, rows, :] = full[i, rows, :] + a
        new = []
        for i, a in enumerate(side_adds(far_cell, own_cell, far_side)):
            c = 24 * n + 6 + i
            extra = jnp.where(lanes == 0, corners[:, c : c + 1], 0.0)
            extra = jnp.where(lanes == 127, corners[:, c + 10 : c + 11], extra)
            new.append(far[5 + i] + a + extra)
        results.append(new)
    later = pressures(results)
    for n, (new, far) in enumerate(zip(results, (south_far, north_far))):
        for i, value in enumerate(new + [far[4] * later[n], far[4]]):
            halo[n, i, pl.ds(0, levels), :] = value

    def beside(value, k, j):
        far_e = pltpu.roll(far_cols[1][j], 127 - k, 1)
        far_w = pltpu.roll(far_cols[0][j], 128 - k, 1)
        return (
            jnp.where(lane == 127, far_e, pltpu.roll(value, 127, 1)),
            jnp.where(lane == 0, far_w, pltpu.roll(value, 1, 1)),
            jnp.where(sub == 7, halo[1, j, pl.ds(k, 1), :], pltpu.roll(value, 7, 0)),
            jnp.where(sub == 0, halo[0, j, pl.ds(k, 1), :], pltpu.roll(value, 1, 0)),
        )

    outs = (temp, salt, east_out, north_out)

    def last(k, total):
        fields = [full[i, tile(k), :] for i in range(4)]
        above = [full[i, tile(k - 1), :] for i in range(4)]
        below = [full[i, tile(k + 1), :] for i in range(4)]
        wet = wet_ref[tile(k), :]
        wet_v = wet_ref[tile(k - 1), :] + wet_ref[tile(k + 1), :]
        dens = density(fields[0], fields[1])
        total = total + dens
        p = GRAVITY * (total - 0.5 * dens)
        new = tile_update(k, fields, above, below, [beside(f, k, i) for i, f in enumerate(fields)], wet, wet_v,
                          beside(wet, k, 5), p, beside(wet * p, k, 4), cor, bat)
        for ref, value in zip(outs, new):
            ref[k] = value
        return total

    levels_loop(levels, last, jnp.zeros((8, 128), jnp.float32))


def shape(*dims):
    return jax.ShapeDtypeStruct(dims, jnp.float32)


def call(kernel, outs, ins, scratch=()):
    vmem = pl.BlockSpec(memory_space=pltpu.VMEM)
    return pl.pallas_call(
        kernel,
        out_shape=outs,
        in_specs=[pl.BlockSpec(memory_space=pltpu.SMEM)] + [vmem] * (len(ins) - 1),
        out_specs=[vmem] * len(outs),
        scratch_shapes=list(scratch),
        compiler_params=pltpu.CompilerParams(vmem_limit_bytes=40 * 2**20),
        cost_estimate=pl.CostEstimate(flops=10**7, bytes_accessed=4 * 10**6, transcendentals=0),
    )(*ins)


def pairs_of(names, count_lon, count_lat):
    def at(lon, lat):
        return lon * count_lat + lat if names[0] == "lon" else lat * count_lon + lon

    every = [(lon, lat) for lon in range(count_lon) for lat in range(count_lat)]
    on = [(at(o, a), at(o ^ 1, a)) for o, a in every]
    off = [(at(o, a), at((o + 1 if o % 2 else o - 1) % count_lon, a)) for o, a in every]
    xs = [(at(o, a), at(o, a ^ 1)) for o, a in every]
    zb = []
    for o, a in every:
        if a == count_lat - 1:
            zb.append((at(o, a), at(count_lon - 1 - o, a)))
        elif a > 0:
            zb.append((at(o, a), at(o, a + 1 if a % 2 else a - 1)))
    return on, off, xs, zb


def per_device(names, count_lon, count_lat, temp, salt, east, north, sea, bathymetry, vorticity):
    levels = temp.shape[0]
    on_pairs, off_pairs, xs_pairs, zb_pairs = pairs_of(names, count_lon, count_lat)
    place = jnp.stack([lax.axis_index("lon"), lax.axis_index("lat")]).astype(jnp.int32)
    tall = 8 * (levels + 2)
    ten = shape(10, 8, 128)
    long = 8 * ((9 * levels + 7) // 8)
    message = shape(long, 128)
    part, wet, xs_own, zb_own, on_own, off_own = call(
        functools.partial(first_kernel, levels),
        [shape(4, tall, 128), shape(tall, 128), message, message, ten, ten],
        [place, temp, salt, east, north, sea, bathymetry, vorticity],
        [pltpu.VMEM((4, tall, 128), jnp.float32), pltpu.VMEM((8 * levels, 128), jnp.float32)],
    )
    move = functools.partial(lax.ppermute, axis_name=names)
    xs = move(xs_own, perm=xs_pairs)
    on = move(on_own, perm=on_pairs)
    off = move(off_own, perm=off_pairs)
    zb = move(zb_own, perm=zb_pairs)
    full, corner_xs, corner_zb = call(
        functools.partial(second_kernel, levels),
        [shape(4, tall, 128), shape(24, 128), shape(24, 128)],
        [place, part, on_own, off_own, on, off],
    )
    corner_xs = move(corner_xs, perm=xs_pairs)
    corner_zb = move(corner_zb, perm=zb_pairs)
    out = shape(levels, 8, 128)
    return tuple(
        call(
            functools.partial(third_kernel, levels, count_lat - 1),
            [out] * 4,
            [place, full, wet, bathymetry, vorticity, xs_own, zb_own, xs, zb, on_own, off_own, on, off,
             corner_xs, corner_zb],
            [
                pltpu.VMEM((4, tall, 128), jnp.float32),
                pltpu.VMEM((2, 6, 8 * ((levels + 7) // 8), 128), jnp.float32),
                pltpu.VMEM((long, 128), jnp.float32),
            ],
        )
    )


def solution(mesh):
    cube, plane = P(None, "lat", "lon"), P("lat", "lon")
    names = tuple(n for n in mesh.axis_names if n in ("lon", "lat"))
    return jax.shard_map(
        functools.partial(per_device, names, mesh.shape["lon"], mesh.shape["lat"]),
        mesh=mesh,
        in_specs=(cube,) * 5 + (plane,) * 2,
        out_specs=(cube,) * 4,
        check_vma=False,
    )
```

profile of v0, /device:TPU:226, one launch (start us, length us, event | category | flops | bytes accessed | tf_op | source)
XLA Modules:
  0.0 63.9 jit_solution(5096853596022255013)
XLA Ops:
  0.6 0.1 pad_add_fusion.place
  0.7 0.0 copy-start
  0.7 1.0 %copy-done = f32[75,8,128]{2,1,0:T(8,128)S(1)} copy-done((f32[75,8,128]{2,1,0:T(8,128)S(1)}, f32[75,8,128]{2,1,0:T(8,128)}, u32[]{:S(2)}) %copy-start) | copy-done | bytes 307224
  1.7 0.0 copy-start.1
  1.7 1.0 %copy-done.1 = f32[75,8,128]{2,1,0:T(8,128)S(1)} copy-done((f32[75,8,128]{2,1,0:T(8,128)S(1)}, f32[75,8,128]{2,1,0:T(8,128)}, u32[]{:S(2)}) %copy-start.1) | copy-done | bytes 307224
  2.6 0.0 copy-start.2
  2.6 1.0 %copy-done.2 = f32[75,8,128]{2,1,0:T(8,128)S(1)} copy-done((f32[75,8,128]{2,1,0:T(8,128)S(1)}, f32[75,8,128]{2,1,0:T(8,128)}, u32[]{:S(2)}) %copy-start.2) | copy-done | bytes 307224
  3.6 0.0 copy-start.3
  3.6 1.0 %copy-done.3 = f32[75,8,128]{2,1,0:T(8,128)S(1)} copy-done((f32[75,8,128]{2,1,0:T(8,128)S(1)}, f32[75,8,128]{2,1,0:T(8,128)}, u32[]{:S(2)}) %copy-start.3) | copy-done | bytes 307224
  4.6 0.0 copy-start.4
  4.6 1.0 %copy-done.4 = s32[75,8,128]{2,1,0:T(8,128)S(1)} copy-done((s32[75,8,128]{2,1,0:T(8,128)S(1)}, s32[75,8,128]{2,1,0:T(8,128)}, u32[]{:S(2)}) %copy-start.4) | copy-done | bytes 307224
  5.5 0.0 copy-start.5
  5.5 0.7 %copy-done.5 = s32[8,128]{1,0:T(8,128)S(1)} copy-done((s32[8,128]{1,0:T(8,128)S(1)}, s32[8,128]{1,0:T(8,128)}, u32[]{:S(2)}) %copy-start.5) | copy-done | bytes 4120
  6.2 0.0 copy-start.6
  6.2 0.7 %copy-done.6 = f32[8,128]{1,0:T(8,128)S(1)} copy-done((f32[8,128]{1,0:T(8,128)S(1)}, f32[8,128]{1,0:T(8,128)}, u32[]{:S(2)}) %copy-start.6) | copy-done | bytes 4120
  6.9 6.3 %shard_map.102 = (f32[4,616,128]{2,1,0:T(8,128)S(1)}, f32[616,128]{1,0:T(8,128)S(1)}, f32[680,128]{1,0:T(8,128)S(1)}, f32[680,128]{1,0:T(8,128)S(1)}, f32[10,8,1...) custom-call(s32[2]{0:T(128)S(1)} %pad_add_fusion.place, f32[75,8,128]{2,1,0:T(8,128)S(1)} %copy-done, ...), custom_call_target="tpu_custom_call" | custom-call | flops 10000000 | bytes 4000000 | tf_op jit(solution)/shard_map/pallas_call | solution.py:340
  13.2 0.6 collective-permute-start.2
  13.8 5.9 %collective-permute-start.3 = (f32[680,128]{1,0:T(8,128)S(1)}, f32[680,128]{1,0:T(8,128)S(1)}, u32[]{:S(2)}, u32[]{:S(2)}) collective-permute-start(f32[680,128]{1,0:T(8,128)S(1)} %get-tuple-element.19.zb_own), channel_id=1, source_target_pairs={{1,2},{2,1},{3,4},{4,3},{5,6},{6,5},{7,8},{8,7},{9,10},{10,9},{11,... | collective-permute-start | bytes 1044488 | tf_op jit(solution)/shard_map/ppermute | solution.py:386
  19.8 1.0 %collective-permute-start = (f32[10,8,128]{2,1,0:T(8,128)S(1)}, f32[10,8,128]{2,1,0:T(8,128)S(1)}, u32[]{:S(2)}, u32[]{:S(2)}) collective-permute-start(f32[10,8,128]{2,1,0:T(8,128)S(1)} %get-tuple-element.14.on_own), channel_id=1, source_target_pairs={{0,16},{1,17},{2,18},{3,19},{4,20},{5,21},{6,22},{7,23},{8,24},{9,... | collective-permute-start | bytes 122888 | tf_op jit(solution)/shard_map/ppermute | solution.py:384
  20.8 0.5 collective-permute-start.1
  21.3 0.4 collective-permute-done.on
  21.7 19.5 %collective-permute-done.1.off = f32[10,8,128]{2,1,0:T(8,128)S(1)} collective-permute-done((f32[10,8,128]{2,1,0:T(8,128)S(1)}, f32[10,8,128]{2,1,0:T(8,128)S(1)}, u32[]{:S(2)}, u32[]{:S(2)}) %collective-permute-start.1) | collective-permute-done | bytes 40992 | tf_op jit(solution)/shard_map/ppermute | solution.py:385
  41.2 2.2 %shard_map.103 = (f32[4,616,128]{2,1,0:T(8,128)S(1)}, f32[24,128]{1,0:T(8,128)S(1)}, f32[24,128]{1,0:T(8,128)S(1)}) custom-call(s32[2]{0:T(128)S(1)} %pad_add_fusion.place, f32[4,616,128]{2,1,0:T(8,128)S(1)} %get-tuple-element.13.part, f32[10,8,128]{2,1,0:T(8,128)S(1)} %get-tuple-element.14.on_own, f32[10,8,128]{2,1,0:T(8,128)S(1)} %get-tuple-element.15.off_own, ...), custom_call_target="tpu_custom_call" | custom-call | flops 10000000 | bytes 4000000 | tf_op jit(solution)/shard_map/pallas_call | solution.py:340
  43.5 0.1 collective-permute-start.4
  43.5 3.3 %collective-permute-start.5 = (f32[24,128]{1,0:T(8,128)S(1)}, f32[24,128]{1,0:T(8,128)S(1)}, u32[]{:S(2)}, u32[]{:S(2)}) collective-permute-start(f32[24,128]{1,0:T(8,128)S(1)} %get-tuple-element.21), channel_id=1, source_target_pairs={{1,2},{2,1},{3,4},{4,3},{5,6},{6,5},{7,8},{8,7},{9,10},{10,9},{11,... | collective-permute-start | bytes 36872 | tf_op jit(solution)/shard_map/ppermute | solution.py:393
  46.8 0.4 collective-permute-done.4.corner_xs
  47.2 4.9 %collective-permute-done.5.corner_zb = f32[24,128]{1,0:T(8,128)S(1)} collective-permute-done((f32[24,128]{1,0:T(8,128)S(1)}, f32[24,128]{1,0:T(8,128)S(1)}, u32[]{:S(2)}, u32[]{:S(2)}) %collective-permute-start.5) | collective-permute-done | bytes 12320 | tf_op jit(solution)/shard_map/ppermute | solution.py:393
  52.2 0.0 collective-permute-done.2.xs
  52.2 0.0 collective-permute-done.3.zb
  52.2 11.7 %shard_map.104 = (f32[75,8,128]{2,1,0:T(8,128)}, f32[75,8,128]{2,1,0:T(8,128)}, f32[75,8,128]{2,1,0:T(8,128)}, f32[75,8,128]{2,1,0:T(8,128)}) custom-call(s32[2]{0:T(128)S(1)} %pad_add_fusion.place, f32[4,616,128]{2,1,0:T(8,128)S(1)} %get-tuple-element.16.full_in, f32[616,128]{1,0:T(8,128)S(1)} %get-tuple-element.17.wet_ref, s32[8,128]{1,0:T(8,128)S(1)} %copy-done.5, ...), custom_call_target="tpu_custom_call" | custom-call | flops 10000000 | bytes 4000000 | tf_op jit(solution)/shard_map/pallas_call | solution.py:340
Async XLA Ops:
  0.7 1.0 %copy-start = (f32[75,8,128]{2,1,0:T(8,128)S(1)}, f32[75,8,128]{2,1,0:T(8,128)}, u32[]{:S(2)}) copy-start(f32[75,8,128]{2,1,0:T(8,128)} %temp.1) | copy-start | bytes 921604
  1.7 1.0 %copy-start.1 = (f32[75,8,128]{2,1,0:T(8,128)S(1)}, f32[75,8,128]{2,1,0:T(8,128)}, u32[]{:S(2)}) copy-start(f32[75,8,128]{2,1,0:T(8,128)} %salt.1) | copy-start | bytes 921604
  2.6 1.0 %copy-start.2 = (f32[75,8,128]{2,1,0:T(8,128)S(1)}, f32[75,8,128]{2,1,0:T(8,128)}, u32[]{:S(2)}) copy-start(f32[75,8,128]{2,1,0:T(8,128)} %east.1) | copy-start | bytes 921604
  3.6 1.0 %copy-start.3 = (f32[75,8,128]{2,1,0:T(8,128)S(1)}, f32[75,8,128]{2,1,0:T(8,128)}, u32[]{:S(2)}) copy-start(f32[75,8,128]{2,1,0:T(8,128)} %north.1) | copy-start | bytes 921604
  4.6 1.0 %copy-start.4 = (s32[75,8,128]{2,1,0:T(8,128)S(1)}, s32[75,8,128]{2,1,0:T(8,128)}, u32[]{:S(2)}) copy-start(s32[75,8,128]{2,1,0:T(8,128)} %sea.1) | copy-start | bytes 921604
  5.5 0.7 %copy-start.5 = (s32[8,128]{1,0:T(8,128)S(1)}, s32[8,128]{1,0:T(8,128)}, u32[]{:S(2)}) copy-start(s32[8,128]{1,0:T(8,128)} %bat_ref.3) | copy-start | bytes 12292
  6.2 0.7 %copy-start.6 = (f32[8,128]{1,0:T(8,128)S(1)}, f32[8,128]{1,0:T(8,128)}, u32[]{:S(2)}) copy-start(f32[8,128]{1,0:T(8,128)} %cor_ref.3) | copy-start | bytes 12292
  13.2 39.0 %collective-permute-start.2 = (f32[680,128]{1,0:T(8,128)S(1)}, f32[680,128]{1,0:T(8,128)S(1)}, u32[]{:S(2)}, u32[]{:S(2)}) collective-permute-start(f32[680,128]{1,0:T(8,128)S(1)} %get-tuple-element.18.xs_own), channel_id=1, source_target_pairs={{0,1},{1,0},{2,3},{3,2},{4,5},{5,4},{6,7},{7,6},{8,9},{9,8},{10,11... | collective-permute-start | bytes 1044488 | tf_op jit(solution)/shard_map/ppermute | solution.py:383
  13.8 38.3 %collective-permute-start.3 = (f32[680,128]{1,0:T(8,128)S(1)}, f32[680,128]{1,0:T(8,128)S(1)}, u32[]{:S(2)}, u32[]{:S(2)}) collective-permute-start(f32[680,128]{1,0:T(8,128)S(1)} %get-tuple-element.19.zb_own), channel_id=1, source_target_pairs={{1,2},{2,1},{3,4},{4,3},{5,6},{6,5},{7,8},{8,7},{9,10},{10,9},{11,... | collective-permute-start | bytes 1044488 | tf_op jit(solution)/shard_map/ppermute | solution.py:386
  19.8 1.9 %collective-permute-start = (f32[10,8,128]{2,1,0:T(8,128)S(1)}, f32[10,8,128]{2,1,0:T(8,128)S(1)}, u32[]{:S(2)}, u32[]{:S(2)}) collective-permute-start(f32[10,8,128]{2,1,0:T(8,128)S(1)} %get-tuple-element.14.on_own), channel_id=1, source_target_pairs={{0,16},{1,17},{2,18},{3,19},{4,20},{5,21},{6,22},{7,23},{8,24},{9,... | collective-permute-start | bytes 122888 | tf_op jit(solution)/shard_map/ppermute | solution.py:384
  20.8 20.4 %collective-permute-start.1 = (f32[10,8,128]{2,1,0:T(8,128)S(1)}, f32[10,8,128]{2,1,0:T(8,128)S(1)}, u32[]{:S(2)}, u32[]{:S(2)}) collective-permute-start(f32[10,8,128]{2,1,0:T(8,128)S(1)} %get-tuple-element.15.off_own), channel_id=1, source_target_pairs={{0,240},{1,241},{2,242},{3,243},{4,244},{5,245},{6,246},{7,247},{8... | collective-permute-start | bytes 122888 | tf_op jit(solution)/shard_map/ppermute | solution.py:385
  43.5 3.8 %collective-permute-start.4 = (f32[24,128]{1,0:T(8,128)S(1)}, f32[24,128]{1,0:T(8,128)S(1)}, u32[]{:S(2)}, u32[]{:S(2)}) collective-permute-start(f32[24,128]{1,0:T(8,128)S(1)} %get-tuple-element.20), channel_id=1, source_target_pairs={{0,1},{1,0},{2,3},{3,2},{4,5},{5,4},{6,7},{7,6},{8,9},{9,8},{10,11... | collective-permute-start | bytes 36872 | tf_op jit(solution)/shard_map/ppermute | solution.py:392
  43.5 8.6 %collective-permute-start.5 = (f32[24,128]{1,0:T(8,128)S(1)}, f32[24,128]{1,0:T(8,128)S(1)}, u32[]{:S(2)}, u32[]{:S(2)}) collective-permute-start(f32[24,128]{1,0:T(8,128)S(1)} %get-tuple-element.21), channel_id=1, source_target_pairs={{1,2},{2,1},{3,4},{4,3},{5,6},{6,5},{7,8},{8,7},{9,10},{10,9},{11,... | collective-permute-start | bytes 36872 | tf_op jit(solution)/shard_map/ppermute | solution.py:393
where the time goes:
time: 64.2 us; the launch traced here: 63.9 us
  waiting for transfers between devices  25.3 us (39%)
  Pallas kernels  20.2 us (31%)
  starting transfers between devices  11.4 us (18%)
  local copies, waits for them, and re-layouts  6.2 us (10%)
  between operations  0.69 us (1%)
    pallas_call x3, Pallas kernels, call(): pl.pallas_call(kernel, out_shape=outs, in_specs=[pl.BlockSpec(memory_spac...  20.2 us
    ppermute x1, waiting for transfers between devices, per_device(): off = move(off_own, perm=off_pairs)  19.5 us
    unnamed x14, local copies, waits for them, and re-layouts  6.2 us
    ppermute x1, starting transfers between devices, per_device(): zb = move(zb_own, perm=zb_pairs)  5.92 us
    ppermute x1, waiting for transfers between devices, per_device(): corner_zb = move(corner_zb, perm=zb_pairs)  4.95 us
    ppermute x1, starting transfers between devices, per_device(): corner_zb = move(corner_zb, perm=zb_pairs)  3.26 us
  transfers between devices with their start and end apart: 6, of which 4 were waited for; matrix products, arithmetic and copies ran while one was open for 0% of the time, Pallas kernels for 3%

commit v1 on v0

v1 whole, which is shorter than its diff:
```python
import functools

import jax
import jax.numpy as jnp
from jax import lax
from jax.experimental import pallas as pl
from jax.experimental.pallas import tpu as pltpu
from jax.sharding import PartitionSpec as P

SIDE = 0.4
STEP = 0.1
THERMAL = 0.2
HALINE = 0.8
GRAVITY = 0.1
DRAG = 2.0
HIGH = lax.Precision.HIGHEST
LOW = 64
UNROLL_A = 5
UNROLL_B = 4
UNROLL_C = 8
UNROLL_D = 4


def levels_loop(first, last, unroll, body, carry):
    count = (last - first) // unroll

    def group(index, carry):
        for step in range(unroll):
            carry = body(first + index * unroll + step, carry)
        return carry

    carry = lax.fori_loop(0, count, group, carry)
    for k in range(first + count * unroll, last):
        carry = body(k, carry)
    return carry


def tile(k):
    return pl.ds(pl.multiple_of(8 * (k + 1), 8), 8)


def density(temp, salt):
    return HALINE * salt - THERMAL * temp


def tile_update(k, fields, above, below, around, wet, wet_v, wet_around, press, press_around, cor, bat, base, half):
    signs = (-1.0, 1.0, -1.0, 1.0)
    speeds = (fields[2], fields[2], fields[3], fields[3])
    ways = [b + v * h if s > 0 else b - v * h for b, h, v, s in zip(base, half, speeds, signs)]
    own = SIDE * wet_v
    for way, wet_n in zip(ways, wet_around):
        own = own + way * wet_n
    tend = []
    for f, up, down, sides in zip(fields, above, below, around):
        t = SIDE * (up + down) - own * f
        for way, q in zip(ways, sides):
            t = t + way * q
        tend.append(t)
    slopes = [h * (m - press * w) for h, m, w in zip(half, press_around, wet_around)]
    rate = jnp.where(bat == lax.convert_element_type(k + 1, jnp.float32), DRAG, 0.0)
    tend[2] = tend[2] + (cor * fields[3] - (slopes[0] - slopes[1]) - rate * fields[2])
    tend[3] = tend[3] - (cor * fields[2] + (slopes[2] - slopes[3]) + rate * fields[3])
    scale = STEP * wet
    return [f + scale * t for f, t in zip(fields, tend)]


def from_side(centre, other, way, to_u, to_v):
    scale = STEP * centre[4]
    wet_n = other[4]
    adds = [scale * (way * (other[i] - wet_n * centre[i])) for i in range(4)]
    push = (0.5 * scale) * (wet_n * (other[5] - centre[5]))
    if to_u:
        adds[2] = adds[2] + to_u * push
    if to_v:
        adds[3] = adds[3] + to_v * push
    return adds


def way_of(cell, side):
    if side == "east":
        return SIDE - 0.5 * cell[2]
    if side == "west":
        return SIDE + 0.5 * cell[2]
    if side == "north":
        return SIDE - 0.5 * cell[3]
    return SIDE + 0.5 * cell[3]


PUSH = {"east": (-1.0, 0.0), "west": (1.0, 0.0), "north": (0.0, -1.0), "south": (0.0, 1.0)}


def side_adds(cell, other, side):
    return from_side(cell, other, way_of(cell, side), *PUSH[side])


def iotas(shape=(8, 128)):
    return lax.broadcasted_iota(jnp.int32, shape, 0), lax.broadcasted_iota(jnp.int32, shape, 1)


def swap(value):
    _, lane = iotas(value.shape)
    return jnp.where(lane % 2 == 0, pltpu.roll(value, 127, 1), pltpu.roll(value, 1, 1))


def level_of(lane, odd):
    return jnp.where(lane % 2 == odd, lane // 2, LOW + lane // 2)


def running(odd):
    row, col = iotas((128, 128))
    row, col = level_of(row, odd), level_of(col, odd)
    return jnp.where(row < col, 1.0, jnp.where(row == col, 0.5, 0.0))


def merged(west, east):
    _, lane = iotas()
    even = lane % 2 == 0
    return (
        [jnp.where(even, w, pltpu.roll(e, 126, 1)) for w, e in zip(west, east)],
        [jnp.where(even, e, w) for w, e in zip(west, east)],
    )


def turn_of(k, high):
    return (127 - 2 * (k - LOW)) if high else (128 - 2 * k)


def first_kernel(levels, place, fields_in, sea, columns_in,
                 part, wet_ref, on, off, state, press):
    lon_odd = place[0] % 2
    sub, lane = iotas()
    bat, cor = columns_in[0], columns_in[1]
    zero = jnp.zeros((8, 128), jnp.float32)
    for i in range(4):
        for edge in (-1, levels):
            state[i, pl.ds(8 * (edge + 1), 8), :] = zero
            part[i, pl.ds(8 * (edge + 1), 8), :] = zero
    for edge in (-1, levels):
        wet_ref[pl.ds(8 * (edge + 1), 8), :] = zero
    pair = lane // 2

    def keep(k, columns, values, high):
        at = k - LOW if high else k
        here = pair == at
        return [jnp.where(here, pltpu.roll(v, 2 * at + 1, 1), c) for c, v in zip(columns, values)]

    def prepare(high, k, carry):
        total, columns = carry
        wet = sea[k]
        fields = [fields_in[i, k] for i in range(4)]
        for i in range(4):
            state[i, tile(k), :] = fields[i]
        wet_ref[tile(k), :] = wet
        dens = density(fields[0], fields[1])
        total = total + dens
        p = GRAVITY * (total - 0.5 * dens)
        press[tile(k), :] = p
        return total, keep(k, columns, fields + [wet, p], high)

    def ranges(first, last):
        parts = [(first, min(last, LOW), False), (max(first, LOW), last, True)]
        return [p for p in parts if p[0] < p[1]]

    total = zero
    columns = {False: [zero] * 6, True: [zero] * 6}
    for first, last, high in ranges(0, levels):
        total, columns[high] = levels_loop(
            first, last, UNROLL_A, functools.partial(prepare, high), (total, columns[high]))

    open_sides = [ok.astype(jnp.float32) for ok in (lane < 127, lane > 0, sub < 7, sub > 0)]
    base = [SIDE * ok for ok in open_sides]
    half = [0.5 * ok for ok in open_sides]

    def beside(value):
        return (pltpu.roll(value, 127, 1), pltpu.roll(value, 1, 1), pltpu.roll(value, 7, 0), pltpu.roll(value, 1, 0))

    def partial(high, k, more):
        fields = [state[i, tile(k), :] for i in range(4)]
        above = [state[i, tile(k - 1), :] for i in range(4)]
        below = [state[i, tile(k + 1), :] for i in range(4)]
        wet = wet_ref[tile(k), :]
        wet_v = wet_ref[tile(k - 1), :] + wet_ref[tile(k + 1), :]
        p = press[tile(k), :]
        new = tile_update(k, fields, above, below, [beside(f) for f in fields], wet, wet_v, beside(wet),
                          p, beside(wet * p), cor, bat, base, half)
        for i in range(4):
            part[i, tile(k), :] = new[i]
        return keep(k, more, new, high)

    more = {False: [zero] * 4, True: [zero] * 4}
    for first, last, high in ranges(0, levels):
        more[high] = levels_loop(first, last, UNROLL_B, functools.partial(partial, high), more[high])

    even = lane % 2 == 0
    for j, (low, high) in enumerate(zip(columns[False] + more[False], columns[True] + more[True])):
        eastern = jnp.where(even, low, pltpu.roll(high, 1, 1))
        west = jnp.where(even, pltpu.roll(high, 127, 1), low)
        on[j] = jnp.where(lon_odd == 0, eastern, west)
        off[j] = jnp.where(lon_odd == 0, west, eastern)


def rows_kernel(levels, place, state, wet_ref, part, xs, zb):
    lat_odd = place[1] % 2
    for ref, row in ((xs, 7 - 7 * lat_odd), (zb, 7 * lat_odd)):
        rows = pl.ds(8 + row, levels, stride=8)
        planes = [state[i, rows, :] for i in range(4)] + [wet_ref[rows, :]] + [part[i, rows, :] for i in range(4)]
        for i, plane in enumerate(planes):
            ref[pl.ds(levels * i, levels), :] = plane
        left = ref.shape[0] - 9 * levels
        if left:
            ref[pl.ds(9 * levels, left), :] = jnp.zeros((left, 128), jnp.float32)


def sides_of(lon_odd, on_own, off_own, on, off):
    odd = lon_odd == 1
    west = [swap(jnp.where(odd, on_own[j], off_own[j])) for j in range(10)]
    east = [swap(jnp.where(odd, off_own[j], on_own[j])) for j in range(10)]
    far_west = [jnp.where(odd, on[j], off[j]) for j in range(10)]
    far_east = [jnp.where(odd, off[j], on[j]) for j in range(10)]
    return west, east, far_west, far_east


def second_kernel(levels, place, part, on_own, off_own, on, off, full, corner_xs, corner_zb):
    lon_odd = place[0] % 2
    lat_odd = place[1] % 2
    _, lane = iotas()
    west, east, far_west, far_east = sides_of(lon_odd, on_own, off_own, on, off)
    adds_w = side_adds(west[:6], far_west[:6], "west")
    adds_e = side_adds(east[:6], far_east[:6], "east")
    entries = far_west[:6] + adds_w + far_east[:6] + adds_e
    for ref, flag in ((corner_xs, lat_odd == 0), (corner_zb, lat_odd == 1)):
        for r, entry in enumerate(entries):
            ref[pl.ds(r, 1), :] = jnp.where(flag, entry[7:8, :], entry[0:1, :])
        ref[pl.ds(20, 4), :] = jnp.zeros((4, 128), jnp.float32)
    ends = (lane == 0) | (lane == 127)

    def add(extra, high, k, carry):
        for i in range(4):
            more = jnp.where(ends, pltpu.roll(extra[i], turn_of(k, high), 1), 0.0)
            full[i, tile(k), :] = part[i, tile(k), :] + more
        return carry

    low, high = merged(adds_w, adds_e)
    levels_loop(0, min(LOW, levels), UNROLL_C, functools.partial(add, low, False), 0)
    if levels > LOW:
        levels_loop(LOW, levels, UNROLL_C, functools.partial(add, high, True), 0)
    zero = jnp.zeros((8, 128), jnp.float32)
    for i in range(4):
        for edge in (-1, levels):
            full[i, pl.ds(8 * (edge + 1), 8), :] = zero


def third_kernel(levels, tops, place, full_in, wet_ref, columns_in, xs_own, zb_own, xs, zb,
                 on_own, off_own, on, off, corner_xs, corner_zb,
                 temp_hbm, salt_hbm, east_hbm, north_hbm, full, halo, flipped, turned, outs, sems):
    lon_odd = place[0] % 2
    lat_odd = place[1] % 2
    odd = lat_odd == 1
    top = place[1] == tops
    sub, lane = iotas()
    bat, cor = columns_in[0], columns_in[1]
    full[...] = full_in[...]

    south_c = jnp.where(odd, corner_xs[...], corner_zb[...])
    north_c = jnp.where(odd, corner_zb[...], corner_xs[...])
    r = lax.broadcasted_iota(jnp.int32, (24, 128), 0)
    swapped = swap(jnp.concatenate([north_c[10:20], north_c[0:10], north_c[20:24]], axis=0))
    s = r % 10
    swapped = jnp.where((s == 2) | (s == 3) | (s == 8) | (s == 9), -swapped, swapped)
    north_c = jnp.where(top, swapped, north_c)

    west, east, far_west, far_east = sides_of(lon_odd, on_own, off_own, on, off)
    far_cols = []
    for own, far, toward, base, order in ((west, far_west, "east", 0, 0), (east, far_east, "west", 10, 1)):
        new = list(far[6:10])
        south_cell = [south_c[base + i : base + i + 1, :] for i in range(6)]
        north_cell = [north_c[base + i : base + i + 1, :] for i in range(6)]
        for i, a in enumerate(side_adds(far[:6], own[:6], toward)):
            new[i] = new[i] + a
        for i, a in enumerate(side_adds(far[:6], south_cell, "south")):
            new[i] = new[i] + jnp.where(sub == 0, a, 0.0)
        for i, a in enumerate(side_adds(far[:6], north_cell, "north")):
            new[i] = new[i] + jnp.where(sub == 7, a, 0.0)
        p = GRAVITY * jnp.dot(density(new[0], new[1]), running(order), precision=HIGH,
                              preferred_element_type=jnp.float32)
        far_cols.append(new + [far[4] * p, far[4]])

    @pl.when(jnp.logical_not(top))
    def _():
        flipped[...] = jnp.where(odd, zb[...], xs[...])

    @pl.when(top)
    def _():
        mirror = 127 - lane
        for t in range(flipped.shape[0] // 8):
            at = pl.ds(8 * t, 8)
            flipped[at, :] = jnp.take_along_axis(zb[at, :], mirror, axis=1, mode="promise_in_bounds")

    def plane(ref, i):
        return ref[pl.ds(levels * i, levels), :]

    sign = jnp.where(top, -1.0, 1.0)
    signs = [1.0, 1.0, sign, sign, 1.0, 1.0, 1.0, sign, sign]
    north_far = [plane(flipped, i) * signs[i] for i in range(9)]
    south_far = [jnp.where(odd, plane(xs, i), plane(zb, i)) for i in range(9)]
    north_own = [jnp.where(odd, plane(zb_own, i), plane(xs_own, i)) for i in range(5)]
    south_own = [jnp.where(odd, plane(xs_own, i), plane(zb_own, i)) for i in range(5)]
    row, col = iotas((levels, levels))
    lower = jnp.where(col < row, 1.0, jnp.where(row == col, 0.5, 0.0))

    def pressures(planes):
        dens = jnp.concatenate([density(f[0], f[1]) for f in planes], axis=1)
        p = GRAVITY * jnp.dot(lower, dens, precision=HIGH, preferred_element_type=jnp.float32)
        return [p[:, 128 * j : 128 * j + 128] for j in range(len(planes))]

    before = pressures([south_far, north_far, south_own, north_own])
    lanes = lax.broadcasted_iota(jnp.int32, (levels, 128), 1)
    turned[...] = jnp.concatenate([south_c, north_c, jnp.zeros((80, 128), jnp.float32)], axis=0).T

    def in_order(odd_first):
        low = min(LOW, levels)
        parts = [turned[pl.ds(odd_first, low, stride=2), :]]
        if levels > LOW:
            parts.append(turned[pl.ds(1 - odd_first, levels - LOW, stride=2), :])
        return jnp.concatenate(parts, axis=0)

    west_c, east_c = in_order(0), in_order(1)
    results = []
    for n, (far, own, own_side, far_side, own_row) in enumerate(
        ((south_far, south_own, "south", "north", 0), (north_far, north_own, "north", "south", 7))
    ):
        far_cell = far[:5] + [before[n]]
        own_cell = own[:5] + [before[2 + n]]
        rows = pl.ds(8 + own_row, levels, stride=8)
        for i, a in enumerate(side_adds(own_cell, far_cell, own_side)):
            full[i, rows, :] = full[i, rows, :] + a
        new = []
        for i, a in enumerate(side_adds(far_cell, own_cell, far_side)):
            c = 24 * n + 6 + i
            extra = jnp.where(lanes == 0, west_c[:, c : c + 1], 0.0)
            extra = jnp.where(lanes == 127, east_c[:, c + 10 : c + 11], extra)
            new.append(far[5 + i] + a + extra)
        results.append(new)
    later = pressures(results)
    for n, (new, far) in enumerate(zip(results, (south_far, north_far))):
        for i, value in enumerate(new + [far[4] * later[n], far[4]]):
            halo[n, i, pl.ds(0, levels), :] = value

    chunk = 25 if levels % 25 == 0 else levels

    def copy_of(i, c):
        rows = pl.ds(c * chunk, chunk)
        target = (temp_hbm, salt_hbm, east_hbm, north_hbm)[i]
        return pltpu.make_async_copy(outs.at[i, rows], target.at[rows], sems.at[i, c])

    def beside(value, k, j, extra, high):
        far = pltpu.roll(extra[j], turn_of(k, high), 1)
        return (
            jnp.where(lane == 127, far, pltpu.roll(value, 127, 1)),
            jnp.where(lane == 0, far, pltpu.roll(value, 1, 1)),
            jnp.where(sub == 7, halo[1, j, pl.ds(k, 1), :], pltpu.roll(value, 7, 0)),
            jnp.where(sub == 0, halo[0, j, pl.ds(k, 1), :], pltpu.roll(value, 1, 0)),
        )

    base = [SIDE] * 4
    half = [0.5] * 4

    def last_step(extra, high, k, total):
        fields = [full[i, tile(k), :] for i in range(4)]
        above = [full[i, tile(k - 1), :] for i in range(4)]
        below = [full[i, tile(k + 1), :] for i in range(4)]
        wet = wet_ref[tile(k), :]
        wet_v = wet_ref[tile(k - 1), :] + wet_ref[tile(k + 1), :]
        dens = density(fields[0], fields[1])
        total = total + dens
        p = GRAVITY * (total - 0.5 * dens)
        new = tile_update(k, fields, above, below, [beside(f, k, i, extra, high) for i, f in enumerate(fields)],
                          wet, wet_v, beside(wet, k, 5, extra, high), p, beside(wet * p, k, 4, extra, high),
                          cor, bat, base, half)
        for i in range(4):
            outs[i, k] = new[i]
        return total

    extras = merged(far_cols[0], far_cols[1])
    total = jnp.zeros((8, 128), jnp.float32)
    for c in range(levels // chunk):
        first, last = c * chunk, (c + 1) * chunk
        for start, stop, high in ((first, min(last, LOW), False), (max(first, LOW), last, True)):
            if start < stop:
                total = levels_loop(start, stop, UNROLL_D, functools.partial(last_step, extras[int(high)], high), total)
        for i in range(4):
            copy_of(i, c).start()
    for c in range(levels // chunk):
        for i in range(4):
            copy_of(i, c).wait()


def shape(*dims):
    return jax.ShapeDtypeStruct(dims, jnp.float32)


def call(kernel, outs, ins, scratch=(), far_ins=(), far_outs=False):
    vmem = pl.BlockSpec(memory_space=pltpu.VMEM)
    hbm = pl.BlockSpec(memory_space=pltpu.HBM)
    return pl.pallas_call(
        kernel,
        out_shape=outs,
        in_specs=[pl.BlockSpec(memory_space=pltpu.SMEM)] + [hbm if i in far_ins else vmem for i in range(1, len(ins))],
        out_specs=[hbm if far_outs else vmem] * len(outs),
        scratch_shapes=list(scratch),
        compiler_params=pltpu.CompilerParams(vmem_limit_bytes=40 * 2**20),
        cost_estimate=pl.CostEstimate(flops=10**11, bytes_accessed=1000, transcendentals=0),
    )(*ins)


def pairs_of(names, count_lon, count_lat):
    def at(lon, lat):
        return lon * count_lat + lat if names[0] == "lon" else lat * count_lon + lon

    every = [(lon, lat) for lon in range(count_lon) for lat in range(count_lat)]
    on = [(at(o, a), at(o ^ 1, a)) for o, a in every]
    off = [(at(o, a), at((o + 1 if o % 2 else o - 1) % count_lon, a)) for o, a in every]
    xs = [(at(o, a), at(o, a ^ 1)) for o, a in every]
    zb = []
    for o, a in every:
        if a == count_lat - 1:
            zb.append((at(o, a), at(count_lon - 1 - o, a)))
        elif a > 0:
            zb.append((at(o, a), at(o, a + 1 if a % 2 else a - 1)))
    return on, off, xs, zb


def per_device(names, count_lon, count_lat, temp, salt, east, north, sea, bathymetry, vorticity):
    levels = temp.shape[0]
    on_pairs, off_pairs, xs_pairs, zb_pairs = pairs_of(names, count_lon, count_lat)
    place = jnp.stack([lax.axis_index("lon"), lax.axis_index("lat")]).astype(jnp.int32)
    tall = 8 * (levels + 2)
    ten = shape(10, 8, 128)
    long = 8 * ((9 * levels + 7) // 8)
    message = shape(long, 128)
    cube = (levels, 8, 128)
    chunks = 3 if levels % 25 == 0 else 1
    level_ids = lax.broadcasted_iota(jnp.int32, sea.shape, 0)
    wet_in = jnp.where(level_ids < bathymetry[None], sea, 0).astype(jnp.float32)
    fields = jnp.stack([temp, salt, east, north]) * wet_in
    columns = jnp.stack([bathymetry.astype(jnp.float32), vorticity])
    part, wet, on_own, off_own, state = call(
        functools.partial(first_kernel, levels),
        [shape(4, tall, 128), shape(tall, 128), ten, ten, shape(4, tall, 128)],
        [place, fields, wet_in, columns],
        [pltpu.VMEM((tall, 128), jnp.float32)],
    )
    move = functools.partial(lax.ppermute, axis_name=names)
    on = move(on_own, perm=on_pairs)
    off = move(off_own, perm=off_pairs)
    xs_own, zb_own = call(functools.partial(rows_kernel, levels), [message] * 2, [place, state, wet, part])
    xs = move(xs_own, perm=xs_pairs)
    zb = move(zb_own, perm=zb_pairs)
    full, corner_xs, corner_zb = call(
        functools.partial(second_kernel, levels),
        [shape(4, tall, 128), shape(24, 128), shape(24, 128)],
        [place, part, on_own, off_own, on, off],
    )
    corner_xs = move(corner_xs, perm=xs_pairs)
    corner_zb = move(corner_zb, perm=zb_pairs)
    out = shape(levels, 8, 128)
    return tuple(
        call(
            functools.partial(third_kernel, levels, count_lat - 1),
            [out] * 4,
            [place, full, wet, columns, xs_own, zb_own, xs, zb, on_own, off_own, on, off,
             corner_xs, corner_zb],
            [
                pltpu.VMEM((4, tall, 128), jnp.float32),
                pltpu.VMEM((2, 6, 8 * ((levels + 7) // 8), 128), jnp.float32),
                pltpu.VMEM((long, 128), jnp.float32),
                pltpu.VMEM((128, 128), jnp.float32),
                pltpu.VMEM((4,) + cube, jnp.float32),
                pltpu.SemaphoreType.DMA((4, chunks)),
            ],
            far_outs=True,
        )
    )


def solution(mesh):
    cube, plane = P(None, "lat", "lon"), P("lat", "lon")
    names = tuple(n for n in mesh.axis_names if n in ("lon", "lat"))
    return jax.shard_map(
        functools.partial(per_device, names, mesh.shape["lon"], mesh.shape["lat"]),
        mesh=mesh,
        in_specs=(cube,) * 5 + (plane,) * 2,
        out_specs=(cube,) * 4,
        check_vma=False,
    )
```

time: 64.2 us -> 48.8 us (0.76)
  the two profiles are of different devices: /device:TPU:226 before, /device:TPU:231 now
where the time goes in v1:
time: 48.8 us; the launch traced here: 48.5 us
  waiting for transfers between devices  15.3 us (31%)
  starting transfers between devices  14.6 us (30%)
  Pallas kernels  14.1 us (29%)
  other arithmetic  3.82 us (8%)
  between operations  0.72 us (1%)
    pallas_call x4, Pallas kernels, call(): pl.pallas_call(kernel, out_shape=outs, in_specs=[pl.BlockSpec(memory_spac...  14.1 us
    ppermute x1, waiting for transfers between devices, per_device(): corner_xs = move(corner_xs, perm=xs_pairs)  9.92 us
    ppermute x1, starting transfers between devices, per_device(): zb = move(zb_own, perm=zb_pairs)  7.2 us
    ppermute x1, waiting for transfers between devices, per_device(): corner_zb = move(corner_zb, perm=zb_pairs)  5.37 us
    ppermute x1, starting transfers between devices, per_device(): corner_zb = move(corner_zb, perm=zb_pairs)  4.35 us
    ppermute x1, starting transfers between devices, per_device(): off = move(off_own, perm=off_pairs)  2.12 us
    another operation x2, other arithmetic, per_device(): columns = jnp.stack([bathymetry.astype(jnp.float32), vorticity])  1.38 us
    mul x1, other arithmetic, per_device(): fields = jnp.stack([temp, salt, east, north]) * wet_in  1.37 us
  transfers between devices with their start and end apart: 6, of which 2 were waited for; matrix products, arithmetic and copies ran while one was open for 0% of the time, Pallas kernels for 5%

profile of v1, /device:TPU:231, one launch (start us, length us, event | category | flops | bytes accessed | tf_op | source)
XLA Modules:
  0.0 48.5 jit_solution(16521457657957281206)
XLA Ops:
  0.6 0.7 %convert_bitcast_fusion = f32[1,8,128]{2,1,0:T(8,128)S(1)} fusion(s32[8,128]{1,0:T(8,128)} %param.12), kind=kLoop, calls=%fused_computation.4 | loop fusion | flops 1024 | bytes 8192 | tf_op jit(solution)/shard_map/stack | solution.py:446
  1.3 1.0 %select_convert_fusion.sea = f32[75,8,128]{2,1,0:T(8,128)S(1)} fusion(s32[75,8,128]{2,1,0:T(8,128)} %param.11, s32[8,128]{1,0:T(8,128)} %param.12), kind=kLoop, calls=%fused_computation.1 | loop fusion | flops 230400 | bytes 618496 | tf_op jit(solution)/shard_map/convert_element_type | solution.py:444
  2.3 0.1 pad_add_fusion.place
  2.4 0.7 %pad_maximum_fusion.columns_in = f32[2,8,128]{2,1,0:T(8,128)S(1)} fusion(f32[1,8,128]{2,1,0:T(8,128)} %bitcast.13, f32[1,8,128]{2,1,0:T(8,128)S(1)} %convert_bitcast_fusion), kind=kLoop, calls=%fused_computation.3 | loop fusion | flops 2048 | bytes 16384 | tf_op jit(solution)/shard_map/stack | solution.py:446
  3.1 0.0 copy-start
  3.1 1.4 %maximum_multiply_fusion.fields_in = f32[4,75,8,128]{3,2,1,0:T(8,128)S(1)} fusion(f32[1,75,8,128]{3,2,1,0:T(8,128)} %bitcast.9, f32[1,75,8,128]{3,2,1,0:T(8,128)} %bitcast.10, f32[1,75,8,128]{3,2,1,0:T(8,128)} %bitcast.11, f32[1,75,8,128]{3,2,1,0:T(8,128)} %bitcast.12, f32[75,8,128]{2,1,0:T(8,128)S(1)} %select_convert_fusion.sea), kind=kLoop, calls=%fused_computation | loop fusion | flops 1228800 | bytes 2764800 | tf_op jit(solution)/shard_map/mul | solution.py:445
  4.5 0.0 copy-done
  4.5 6.1 %shard_map.102 = (f32[4,616,128]{2,1,0:T(8,128)S(1)}, f32[616,128]{1,0:T(8,128)S(1)}, f32[10,8,128]{2,1,0:T(8,128)S(1)}, f32[10,8,128]{2,1,0:T(8,128)S(1)}, f32[4,616,128]{2,1,0:T(8,128)S(1)}) custom-call(s32[2]{0:T(128)S(1)} %pad_add_fusion.place, f32[4,75,8,128]{3,2,1,0:T(8,128)S(1)} %maximum_multiply_fusion.fields_in, ...), custom_call_target="tpu_custom_call" | custom-call | flops 99999997952 | bytes 1000 | tf_op jit(solution)/shard_map/pallas_call | solution.py:405
  10.6 0.7 %collective-permute-start = (f32[10,8,128]{2,1,0:T(8,128)S(1)}, f32[10,8,128]{2,1,0:T(8,128)S(1)}, u32[]{:S(2)}, u32[]{:S(2)}) collective-permute-start(f32[10,8,128]{2,1,0:T(8,128)S(1)} %get-tuple-element.15.on_own), channel_id=1, source_target_pairs={{0,16},{1,17},{2,18},{3,19},{4,20},{5,21},{6,22},{7,23},{8,24},{9,... | collective-permute-start | bytes 122888 | tf_op jit(solution)/shard_map/ppermute | solution.py:454
  11.3 2.1 %collective-permute-start.1 = (f32[10,8,128]{2,1,0:T(8,128)S(1)}, f32[10,8,128]{2,1,0:T(8,128)S(1)}, u32[]{:S(2)}, u32[]{:S(2)}) collective-permute-start(f32[10,8,128]{2,1,0:T(8,128)S(1)} %get-tuple-element.16.off_own), channel_id=1, source_target_pairs={{0,240},{1,241},{2,242},{3,243},{4,244},{5,245},{6,246},{7,247},{8... | collective-permute-start | bytes 122888 | tf_op jit(solution)/shard_map/ppermute | solution.py:455
  13.4 0.7 %shard_map.104 = (f32[680,128]{1,0:T(8,128)S(1)}, f32[680,128]{1,0:T(8,128)S(1)}) custom-call(s32[2]{0:T(128)S(1)} %pad_add_fusion.place, f32[4,616,128]{2,1,0:T(8,128)S(1)} %get-tuple-element.19.state, f32[616,128]{1,0:T(8,128)S(1)} %get-tuple-element.18.wet_ref, f32[4,616,128]{2,1,0:T(8,128)S(1)} %get-tuple-element.14.part), custom_call_target="tpu_custom_call" | custom-call | flops 99999997952 | bytes 1000 | tf_op jit(solution)/shard_map/pallas_call | solution.py:405
  14.2 0.1 collective-permute-start.2
  14.3 0.0 copy-start.1
  14.3 7.2 %collective-permute-start.3 = (f32[680,128]{1,0:T(8,128)S(1)}, f32[680,128]{1,0:T(8,128)S(1)}, u32[]{:S(2)}, u32[]{:S(2)}) collective-permute-start(f32[680,128]{1,0:T(8,128)S(1)} %get-tuple-element.21.zb_own), channel_id=1, source_target_pairs={{1,2},{2,1},{3,4},{4,3},{5,6},{6,5},{7,8},{8,7},{9,10},{10,9},{11,... | collective-permute-start | bytes 1044488 | tf_op jit(solution)/shard_map/ppermute | solution.py:458
  21.5 0.0 collective-permute-done.on
  21.5 0.0 collective-permute-done.1.off
  21.5 1.6 %shard_map.103 = (f32[4,616,128]{2,1,0:T(8,128)S(1)}, f32[24,128]{1,0:T(8,128)S(1)}, f32[24,128]{1,0:T(8,128)S(1)}) custom-call(s32[2]{0:T(128)S(1)} %pad_add_fusion.place, f32[4,616,128]{2,1,0:T(8,128)S(1)} %get-tuple-element.14.part, f32[10,8,128]{2,1,0:T(8,128)S(1)} %get-tuple-element.15.on_own, f32[10,8,128]{2,1,0:T(8,128)S(1)} %get-tuple-element.16.off_own, ...), custom_call_target="tpu_custom_call" | custom-call | flops 99999997952 | bytes 1000 | tf_op jit(solution)/shard_map/pallas_call | solution.py:405
  23.1 0.1 collective-permute-start.4
  23.2 4.4 %collective-permute-start.5 = (f32[24,128]{1,0:T(8,128)S(1)}, f32[24,128]{1,0:T(8,128)S(1)}, u32[]{:S(2)}, u32[]{:S(2)}) collective-permute-start(f32[24,128]{1,0:T(8,128)S(1)} %get-tuple-element.23), channel_id=1, source_target_pairs={{1,2},{2,1},{3,4},{4,3},{5,6},{6,5},{7,8},{8,7},{9,10},{10,9},{11,... | collective-permute-start | bytes 36872 | tf_op jit(solution)/shard_map/ppermute | solution.py:465
  27.5 9.9 %collective-permute-done.4.corner_xs = f32[24,128]{1,0:T(8,128)S(1)} collective-permute-done((f32[24,128]{1,0:T(8,128)S(1)}, f32[24,128]{1,0:T(8,128)S(1)}, u32[]{:S(2)}, u32[]{:S(2)}) %collective-permute-start.4) | collective-permute-done | bytes 12320 | tf_op jit(solution)/shard_map/ppermute | solution.py:464
  37.4 5.4 %collective-permute-done.5.corner_zb = f32[24,128]{1,0:T(8,128)S(1)} collective-permute-done((f32[24,128]{1,0:T(8,128)S(1)}, f32[24,128]{1,0:T(8,128)S(1)}, u32[]{:S(2)}, u32[]{:S(2)}) %collective-permute-start.5) | collective-permute-done | bytes 12320 | tf_op jit(solution)/shard_map/ppermute | solution.py:465
  42.8 0.0 collective-permute-done.2.xs
  42.8 0.0 collective-permute-done.3.zb
  42.8 0.0 copy-done.1
  42.8 5.7 %shard_map.105 = (f32[75,8,128]{2,1,0:T(8,128)}, f32[75,8,128]{2,1,0:T(8,128)}, f32[75,8,128]{2,1,0:T(8,128)}, f32[75,8,128]{2,1,0:T(8,128)}) custom-call(s32[2]{0:T(128)S(1)} %pad_add_fusion.place, f32[4,616,128]{2,1,0:T(8,128)S(1)} %get-tuple-element.17.full_in, f32[616,128]{1,0:T(8,128)S(1)} %get-tuple-element.18.wet_ref, f32[2,8,128]{2,1,0:T(8,128)S(1)} %copy-done.1, ...), custom_call_target="tpu_custom_call" | custom-call | flops 99999997952 | bytes 1000 | tf_op jit(solution)/shard_map/pallas_call | solution.py:405
Async XLA Ops:
  3.1 1.4 %copy-start = (f32[2,8,128]{2,1,0:T(8,128)}, f32[2,8,128]{2,1,0:T(8,128)S(1)}, u32[]{:S(2)}) copy-start(f32[2,8,128]{2,1,0:T(8,128)S(1)} %pad_maximum_fusion.columns_in) | copy-start | bytes 24580
  10.6 10.9 %collective-permute-start = (f32[10,8,128]{2,1,0:T(8,128)S(1)}, f32[10,8,128]{2,1,0:T(8,128)S(1)}, u32[]{:S(2)}, u32[]{:S(2)}) collective-permute-start(f32[10,8,128]{2,1,0:T(8,128)S(1)} %get-tuple-element.15.on_own), channel_id=1, source_target_pairs={{0,16},{1,17},{2,18},{3,19},{4,20},{5,21},{6,22},{7,23},{8,24},{9,... | collective-permute-start | bytes 122888 | tf_op jit(solution)/shard_map/ppermute | solution.py:454
  11.3 10.2 %collective-permute-start.1 = (f32[10,8,128]{2,1,0:T(8,128)S(1)}, f32[10,8,128]{2,1,0:T(8,128)S(1)}, u32[]{:S(2)}, u32[]{:S(2)}) collective-permute-start(f32[10,8,128]{2,1,0:T(8,128)S(1)} %get-tuple-element.16.off_own), channel_id=1, source_target_pairs={{0,240},{1,241},{2,242},{3,243},{4,244},{5,245},{6,246},{7,247},{8... | collective-permute-start | bytes 122888 | tf_op jit(solution)/shard_map/ppermute | solution.py:455
  14.2 28.6 %collective-permute-start.2 = (f32[680,128]{1,0:T(8,128)S(1)}, f32[680,128]{1,0:T(8,128)S(1)}, u32[]{:S(2)}, u32[]{:S(2)}) collective-permute-start(f32[680,128]{1,0:T(8,128)S(1)} %get-tuple-element.20.xs_own), channel_id=1, source_target_pairs={{0,1},{1,0},{2,3},{3,2},{4,5},{5,4},{6,7},{7,6},{8,9},{9,8},{10,11... | collective-permute-start | bytes 1044488 | tf_op jit(solution)/shard_map/ppermute | solution.py:457
  14.3 28.6 %copy-start.1 = (f32[2,8,128]{2,1,0:T(8,128)S(1)}, f32[2,8,128]{2,1,0:T(8,128)}, u32[]{:S(2)}) copy-start(f32[2,8,128]{2,1,0:T(8,128)} %copy-done) | copy-start | bytes 24580
  14.3 28.5 %collective-permute-start.3 = (f32[680,128]{1,0:T(8,128)S(1)}, f32[680,128]{1,0:T(8,128)S(1)}, u32[]{:S(2)}, u32[]{:S(2)}) collective-permute-start(f32[680,128]{1,0:T(8,128)S(1)} %get-tuple-element.21.zb_own), channel_id=1, source_target_pairs={{1,2},{2,1},{3,4},{4,3},{5,6},{6,5},{7,8},{8,7},{9,10},{10,9},{11,... | collective-permute-start | bytes 1044488 | tf_op jit(solution)/shard_map/ppermute | solution.py:458
  23.1 14.4 %collective-permute-start.4 = (f32[24,128]{1,0:T(8,128)S(1)}, f32[24,128]{1,0:T(8,128)S(1)}, u32[]{:S(2)}, u32[]{:S(2)}) collective-permute-start(f32[24,128]{1,0:T(8,128)S(1)} %get-tuple-element.22), channel_id=1, source_target_pairs={{0,1},{1,0},{2,3},{3,2},{4,5},{5,4},{6,7},{7,6},{8,9},{9,8},{10,11... | collective-permute-start | bytes 36872 | tf_op jit(solution)/shard_map/ppermute | solution.py:464
  23.2 19.6 %collective-permute-start.5 = (f32[24,128]{1,0:T(8,128)S(1)}, f32[24,128]{1,0:T(8,128)S(1)}, u32[]{:S(2)}, u32[]{:S(2)}) collective-permute-start(f32[24,128]{1,0:T(8,128)S(1)} %get-tuple-element.23), channel_id=1, source_target_pairs={{1,2},{2,1},{3,4},{4,3},{5,6},{6,5},{7,8},{8,7},{9,10},{10,9},{11,... | collective-permute-start | bytes 36872 | tf_op jit(solution)/shard_map/ppermute | solution.py:465

commit v2 on v1

--- a/solution.py
+++ b/solution.py
@@ -16,9 +16,13 @@
 HIGH = lax.Precision.HIGHEST
 LOW = 64
 UNROLL_A = 5
-UNROLL_B = 4
-UNROLL_C = 8
-UNROLL_D = 4
+UNROLL_B = 15
+UNROLL_C = 16
+UNROLL_D = 25
+PART = 344
+W_ROWS = 10**11
+W_CORNER = 10**11
+W_ADD = 10**12
 
 
 def levels_loop(first, last, unroll, body, carry):
@@ -125,11 +129,28 @@
     return (127 - 2 * (k - LOW)) if high else (128 - 2 * k)
 
 
-def first_kernel(levels, place, fields_in, sea, columns_in,
-                 part, wet_ref, on, off, state, press):
+def first_kernel(levels, place, temp_hbm, salt_hbm, east_hbm, north_hbm, sea_hbm, bat_hbm, cor_hbm,
+                 part, wet_ref, on, off, state, planes, press, temp, salt, east, north, sea, bat_ref, sems, plane_sems):
+    chunk = 25 if levels % 25 == 0 else levels
+    chunks = levels // chunk
+    inputs = ((temp_hbm, temp), (salt_hbm, salt), (east_hbm, east), (north_hbm, north), (sea_hbm, sea))
+
+    def copy_of(i, c):
+        source, target = inputs[i]
+        rows = pl.ds(c * chunk, chunk)
+        return pltpu.make_async_copy(source.at[rows], target.at[rows], sems.at[i, c])
+
+    plane_copies = [
+        pltpu.make_async_copy(bat_hbm, bat_ref, plane_sems.at[0]),
+        pltpu.make_async_copy(cor_hbm, planes.at[1], plane_sems.at[1]),
+    ]
+    for copy in plane_copies:
+        copy.start()
+    for c in range(chunks):
+        for i in range(5):
+            copy_of(i, c).start()
     lon_odd = place[0] % 2
     sub, lane = iotas()
-    bat, cor = columns_in[0], columns_in[1]
     zero = jnp.zeros((8, 128), jnp.float32)
     for i in range(4):
         for edge in (-1, levels):
@@ -137,35 +158,29 @@
             part[i, pl.ds(8 * (edge + 1), 8), :] = zero
     for edge in (-1, levels):
         wet_ref[pl.ds(8 * (edge + 1), 8), :] = zero
-    pair = lane // 2
-
-    def keep(k, columns, values, high):
-        at = k - LOW if high else k
-        here = pair == at
-        return [jnp.where(here, pltpu.roll(v, 2 * at + 1, 1), c) for c, v in zip(columns, values)]
-
-    def prepare(high, k, carry):
-        total, columns = carry
-        wet = sea[k]
-        fields = [fields_in[i, k] for i in range(4)]
+    for copy in plane_copies:
+        copy.wait()
+    depth = bat_ref[...]
+    bat = depth.astype(jnp.float32)
+    planes[0] = bat
+    cor = planes[1]
+
+    def prepare(k, total):
+        wet = jnp.where(k < depth, sea[k], 0).astype(jnp.float32)
+        fields = [ref[k] * wet for ref in (temp, salt, east, north)]
         for i in range(4):
             state[i, tile(k), :] = fields[i]
         wet_ref[tile(k), :] = wet
         dens = density(fields[0], fields[1])
         total = total + dens
-        p = GRAVITY * (total - 0.5 * dens)
-        press[tile(k), :] = p
-        return total, keep(k, columns, fields + [wet, p], high)
-
-    def ranges(first, last):
-        parts = [(first, min(last, LOW), False), (max(first, LOW), last, True)]
-        return [p for p in parts if p[0] < p[1]]
+        press[tile(k), :] = GRAVITY * (total - 0.5 * dens)
+        return total
 
     total = zero
-    columns = {False: [zero] * 6, True: [zero] * 6}
-    for first, last, high in ranges(0, levels):
-        total, columns[high] = levels_loop(
-            first, last, UNROLL_A, functools.partial(prepare, high), (total, columns[high]))
+    for c in range(chunks):
+        for i in range(5):
+            copy_of(i, c).wait()
+        total = levels_loop(c * chunk, (c + 1) * chunk, UNROLL_A, prepare, total)
 
     open_sides = [ok.astype(jnp.float32) for ok in (lane < 127, lane > 0, sub < 7, sub > 0)]
     base = [SIDE * ok for ok in open_sides]
@@ -174,7 +189,7 @@
     def beside(value):
         return (pltpu.roll(value, 127, 1), pltpu.roll(value, 1, 1), pltpu.roll(value, 7, 0), pltpu.roll(value, 1, 0))
 
-    def partial(high, k, more):
+    def partial(k, carry):
         fields = [state[i, tile(k), :] for i in range(4)]
         above = [state[i, tile(k - 1), :] for i in range(4)]
         below = [state[i, tile(k + 1), :] for i in range(4)]
@@ -185,30 +200,54 @@
                           p, beside(wet * p), cor, bat, base, half)
         for i in range(4):
             part[i, tile(k), :] = new[i]
-        return keep(k, more, new, high)
-
-    more = {False: [zero] * 4, True: [zero] * 4}
-    for first, last, high in ranges(0, levels):
-        more[high] = levels_loop(first, last, UNROLL_B, functools.partial(partial, high), more[high])
-
+        return carry
+
+    levels_loop(0, levels, UNROLL_B, partial, 0)
+
+    pair = lane // 2
+    packed = {}
+    for first, last in ((0, min(LOW, levels)), (LOW, levels)):
+        columns = [zero] * 10
+        for k in range(first, last):
+            here = pair == k - first
+            at = pl.ds(8 * (k + 1), 8)
+            values = [state[i, at, :] for i in range(4)] + [wet_ref[at, :], press[at, :]]
+            values = values + [part[i, at, :] for i in range(4)]
+            columns = [jnp.where(here, pltpu.roll(v, 2 * (k - first) + 1, 1), c) for v, c in zip(values, columns)]
+        packed[first] = columns
     even = lane % 2 == 0
-    for j, (low, high) in enumerate(zip(columns[False] + more[False], columns[True] + more[True])):
+    for j, (low, high) in enumerate(zip(packed[0], packed[LOW])):
         eastern = jnp.where(even, low, pltpu.roll(high, 1, 1))
         west = jnp.where(even, pltpu.roll(high, 127, 1), low)
         on[j] = jnp.where(lon_odd == 0, eastern, west)
         off[j] = jnp.where(lon_odd == 0, west, eastern)
 
 
-def rows_kernel(levels, place, state, wet_ref, part, xs, zb):
+def write_rows(levels, ref, row, state, wet_ref, part):
+    rows = pl.ds(8 + row, levels, stride=8)
+    planes = [state[i, rows, :] for i in range(4)] + [wet_ref[rows, :]] + [part[i, rows, :] for i in range(4)]
+    for i, plane in enumerate(planes):
+        ref[pl.ds(levels * i, levels), :] = plane
+    left = long_of(levels) - 9 * levels
+    if left:
+        ref[pl.ds(9 * levels, left), :] = jnp.zeros((left, 128), jnp.float32)
+
+
+def long_of(levels):
+    return 8 * ((9 * levels + 7) // 8)
+
+
+def rows_kernel(levels, tops, place, state, wet_ref, part, xs, fold_a):
     lat_odd = place[1] % 2
-    for ref, row in ((xs, 7 - 7 * lat_odd), (zb, 7 * lat_odd)):
-        rows = pl.ds(8 + row, levels, stride=8)
-        planes = [state[i, rows, :] for i in range(4)] + [wet_ref[rows, :]] + [part[i, rows, :] for i in range(4)]
+    write_rows(levels, xs, 7 - 7 * lat_odd, state, wet_ref, part)
+
+    @pl.when(place[1] == tops)
+    def _():
+        rows = pl.ds(8 + 7, levels, stride=8)
+        planes = [state[i, rows, :] for i in range(4)] + [wet_ref[rows, :]]
         for i, plane in enumerate(planes):
-            ref[pl.ds(levels * i, levels), :] = plane
-        left = ref.shape[0] - 9 * levels
-        if left:
-            ref[pl.ds(9 * levels, left), :] = jnp.zeros((left, 128), jnp.float32)
+            count = min(levels, PART - levels * i)
+            fold_a[pl.ds(levels * i, count), :] = plane[:count]
 
 
 def sides_of(lon_odd, on_own, off_own, on, off):
@@ -220,18 +259,30 @@
     return west, east, far_west, far_east
 
 
-def second_kernel(levels, place, part, on_own, off_own, on, off, full, corner_xs, corner_zb):
+def corner_kernel(levels, tops, place, on_own, off_own, on, off, state, wet_ref, part, xs_own, zb, fold_b, corner_xs, extra):
     lon_odd = place[0] % 2
     lat_odd = place[1] % 2
-    _, lane = iotas()
+    write_rows(levels, zb, 7 * lat_odd, state, wet_ref, part)
     west, east, far_west, far_east = sides_of(lon_odd, on_own, off_own, on, off)
     adds_w = side_adds(west[:6], far_west[:6], "west")
     adds_e = side_adds(east[:6], far_east[:6], "east")
     entries = far_west[:6] + adds_w + far_east[:6] + adds_e
-    for ref, flag in ((corner_xs, lat_odd == 0), (corner_zb, lat_odd == 1)):
+    for ref, start, flag in ((corner_xs, 0, lat_odd == 0), (zb, long_of(levels), lat_odd == 1)):
         for r, entry in enumerate(entries):
-            ref[pl.ds(r, 1), :] = jnp.where(flag, entry[7:8, :], entry[0:1, :])
-        ref[pl.ds(20, 4), :] = jnp.zeros((4, 128), jnp.float32)
+            ref[pl.ds(start + r, 1), :] = jnp.where(flag, entry[7:8, :], entry[0:1, :])
+        ref[pl.ds(start + 20, 4), :] = jnp.zeros((4, 128), jnp.float32)
+    low, high = merged(adds_w, adds_e)
+    for i in range(4):
+        extra[i] = low[i]
+        extra[4 + i] = high[i]
+
+    @pl.when(place[1] == tops)
+    def _():
+        fold_b[...] = zb[pl.ds(PART, zb.shape[0] - PART), :]
+
+
+def second_kernel(levels, place, part, extra, xs, fold_a, full):
+    _, lane = iotas()
     ends = (lane == 0) | (lane == 127)
 
     def add(extra, high, k, carry):
@@ -240,18 +291,17 @@
             full[i, tile(k), :] = part[i, tile(k), :] + more
         return carry
 
-    low, high = merged(adds_w, adds_e)
-    levels_loop(0, min(LOW, levels), UNROLL_C, functools.partial(add, low, False), 0)
+    levels_loop(0, min(LOW, levels), UNROLL_C, functools.partial(add, [extra[i] for i in range(4)], False), 0)
     if levels > LOW:
-        levels_loop(LOW, levels, UNROLL_C, functools.partial(add, high, True), 0)
+        levels_loop(LOW, levels, UNROLL_C, functools.partial(add, [extra[4 + i] for i in range(4)], True), 0)
     zero = jnp.zeros((8, 128), jnp.float32)
     for i in range(4):
         for edge in (-1, levels):
             full[i, pl.ds(8 * (edge + 1), 8), :] = zero
 
 
-def third_kernel(levels, tops, place, full_in, wet_ref, columns_in, xs_own, zb_own, xs, zb,
-                 on_own, off_own, on, off, corner_xs, corner_zb,
+def third_kernel(levels, tops, place, full_in, wet_ref, columns_in, xs_own, zb_own, xs, zb, fold_a, fold_b,
+                 on_own, off_own, on, off, corner_xs,
                  temp_hbm, salt_hbm, east_hbm, north_hbm, full, halo, flipped, turned, outs, sems):
     lon_odd = place[0] % 2
     lat_odd = place[1] % 2
@@ -261,8 +311,9 @@
     bat, cor = columns_in[0], columns_in[1]
     full[...] = full_in[...]
 
-    south_c = jnp.where(odd, corner_xs[...], corner_zb[...])
-    north_c = jnp.where(odd, corner_zb[...], corner_xs[...])
+    at_end = pl.ds(long_of(levels), 24)
+    south_c = jnp.where(odd, corner_xs[...], zb[at_end, :])
+    north_c = jnp.where(odd, jnp.where(top, fold_b[pl.ds(long_of(levels) - PART, 24), :], zb[at_end, :]), corner_xs[...])
     r = lax.broadcasted_iota(jnp.int32, (24, 128), 0)
     swapped = swap(jnp.concatenate([north_c[10:20], north_c[0:10], north_c[20:24]], axis=0))
     s = r % 10
@@ -287,14 +338,15 @@
 
     @pl.when(jnp.logical_not(top))
     def _():
-        flipped[...] = jnp.where(odd, zb[...], xs[...])
+        flipped[...] = jnp.where(odd, zb[pl.ds(0, long_of(levels)), :], xs[...])
 
     @pl.when(top)
     def _():
         mirror = 127 - lane
         for t in range(flipped.shape[0] // 8):
-            at = pl.ds(8 * t, 8)
-            flipped[at, :] = jnp.take_along_axis(zb[at, :], mirror, axis=1, mode="promise_in_bounds")
+            at = 8 * t
+            rows = fold_a[pl.ds(at, 8), :] if at < PART else fold_b[pl.ds(at - PART, 8), :]
+            flipped[pl.ds(at, 8), :] = jnp.take_along_axis(rows, mirror, axis=1, mode="promise_in_bounds")
 
     def plane(ref, i):
         return ref[pl.ds(levels * i, levels), :]
@@ -399,7 +451,7 @@
     return jax.ShapeDtypeStruct(dims, jnp.float32)
 
 
-def call(kernel, outs, ins, scratch=(), far_ins=(), far_outs=False):
+def call(kernel, outs, ins, scratch=(), far_ins=(), far_outs=False, work=10**11):
     vmem = pl.BlockSpec(memory_space=pltpu.VMEM)
     hbm = pl.BlockSpec(memory_space=pltpu.HBM)
     return pl.pallas_call(
@@ -408,8 +460,8 @@
         in_specs=[pl.BlockSpec(memory_space=pltpu.SMEM)] + [hbm if i in far_ins else vmem for i in range(1, len(ins))],
         out_specs=[hbm if far_outs else vmem] * len(outs),
         scratch_shapes=list(scratch),
-        compiler_params=pltpu.CompilerParams(vmem_limit_bytes=40 * 2**20),
-        cost_estimate=pl.CostEstimate(flops=10**11, bytes_accessed=1000, transcendentals=0),
+        compiler_params=pltpu.CompilerParams(vmem_limit_bytes=20 * 2**20),
+        cost_estimate=pl.CostEstimate(flops=work, bytes_accessed=1000, transcendentals=0),
     )(*ins)
 
 
@@ -421,55 +473,63 @@
     on = [(at(o, a), at(o ^ 1, a)) for o, a in every]
     off = [(at(o, a), at((o + 1 if o % 2 else o - 1) % count_lon, a)) for o, a in every]
     xs = [(at(o, a), at(o, a ^ 1)) for o, a in every]
-    zb = []
-    for o, a in every:
-        if a == count_lat - 1:
-            zb.append((at(o, a), at(count_lon - 1 - o, a)))
-        elif a > 0:
-            zb.append((at(o, a), at(o, a + 1 if a % 2 else a - 1)))
-    return on, off, xs, zb
+    zb = [(at(o, a), at(o, a + 1 if a % 2 else a - 1)) for o, a in every if 0 < a < count_lat - 1]
+    top = count_lat - 1
+    to_relay = [(at(o, top), at(count_lon - 1 - o, top - 1)) for o in range(count_lon)]
+    from_relay = [(at(o, top - 1), at(o, top)) for o in range(count_lon)]
+    return on, off, xs, zb, to_relay, from_relay
 
 
 def per_device(names, count_lon, count_lat, temp, salt, east, north, sea, bathymetry, vorticity):
     levels = temp.shape[0]
-    on_pairs, off_pairs, xs_pairs, zb_pairs = pairs_of(names, count_lon, count_lat)
+    on_pairs, off_pairs, xs_pairs, zb_pairs, to_relay, from_relay = pairs_of(names, count_lon, count_lat)
     place = jnp.stack([lax.axis_index("lon"), lax.axis_index("lat")]).astype(jnp.int32)
     tall = 8 * (levels + 2)
     ten = shape(10, 8, 128)
-    long = 8 * ((9 * levels + 7) // 8)
+    long = long_of(levels)
     message = shape(long, 128)
     cube = (levels, 8, 128)
     chunks = 3 if levels % 25 == 0 else 1
-    level_ids = lax.broadcasted_iota(jnp.int32, sea.shape, 0)
-    wet_in = jnp.where(level_ids < bathymetry[None], sea, 0).astype(jnp.float32)
-    fields = jnp.stack([temp, salt, east, north]) * wet_in
-    columns = jnp.stack([bathymetry.astype(jnp.float32), vorticity])
-    part, wet, on_own, off_own, state = call(
+    raw = [pltpu.with_memory_space_constraint(x, pltpu.HBM) for x in (temp, salt, east, north, sea, bathymetry, vorticity)]
+    part, wet, on_own, off_own, state, columns = call(
         functools.partial(first_kernel, levels),
-        [shape(4, tall, 128), shape(tall, 128), ten, ten, shape(4, tall, 128)],
-        [place, fields, wet_in, columns],
-        [pltpu.VMEM((tall, 128), jnp.float32)],
+        [shape(4, tall, 128), shape(tall, 128), ten, ten, shape(4, tall, 128), shape(2, 8, 128)],
+        [place, *raw],
+        [pltpu.VMEM((tall, 128), jnp.float32)] + [pltpu.VMEM(cube, jnp.float32)] * 4
+        + [pltpu.VMEM(cube, jnp.int32), pltpu.VMEM((8, 128), jnp.int32), pltpu.SemaphoreType.DMA((5, chunks)),
+           pltpu.SemaphoreType.DMA((2,))],
+        far_ins=(1, 2, 3, 4, 5, 6, 7),
     )
     move = functools.partial(lax.ppermute, axis_name=names)
     on = move(on_own, perm=on_pairs)
     off = move(off_own, perm=off_pairs)
-    xs_own, zb_own = call(functools.partial(rows_kernel, levels), [message] * 2, [place, state, wet, part])
+    xs_own, fold_a = call(
+        functools.partial(rows_kernel, levels, count_lat - 1),
+        [message, shape(PART, 128)],
+        [place, state, wet, part],
+        work=W_ROWS,
+    )
+    fold_a = move(fold_a, perm=to_relay)
     xs = move(xs_own, perm=xs_pairs)
+    zb_own, fold_b, corner_xs, extra = call(
+        functools.partial(corner_kernel, levels, count_lat - 1),
+        [shape(long + 24, 128), shape(long + 24 - PART, 128), shape(24, 128), shape(8, 8, 128)],
+        [place, on_own, off_own, on, off, state, wet, part, xs_own],
+        work=W_CORNER,
+    )
+    fold_b = move(fold_b, perm=to_relay)
     zb = move(zb_own, perm=zb_pairs)
-    full, corner_xs, corner_zb = call(
-        functools.partial(second_kernel, levels),
-        [shape(4, tall, 128), shape(24, 128), shape(24, 128)],
-        [place, part, on_own, off_own, on, off],
-    )
     corner_xs = move(corner_xs, perm=xs_pairs)
-    corner_zb = move(corner_zb, perm=zb_pairs)
+    fold_a = move(fold_a, perm=from_relay)
+    fold_b = move(fold_b, perm=from_relay)
+    full, = call(functools.partial(second_kernel, levels), [shape(4, tall, 128)], [place, part, extra, xs, fold_a], work=W_ADD)
     out = shape(levels, 8, 128)
     return tuple(
         call(
             functools.partial(third_kernel, levels, count_lat - 1),
             [out] * 4,
-            [place, full, wet, columns, xs_own, zb_own, xs, zb, on_own, off_own, on, off,
-             corner_xs, corner_zb],
+            [place, full, wet, columns, xs_own, zb_own, xs, zb, fold_a, fold_b, on_own, off_own, on, off,
+             corner_xs],
             [
                 pltpu.VMEM((4, tall, 128), jnp.float32),
                 pltpu.VMEM((2, 6, 8 * ((levels + 7) // 8), 128), jnp.float32),

time: 48.8 us -> 42.2 us (0.86)
  the two profiles are of different devices: /device:TPU:231 before, /device:TPU:224 now
where the time goes in v2:
time: 42.2 us; the launch traced here: 41.9 us
  starting transfers between devices  19.2 us (45%)
  Pallas kernels  12.6 us (30%)
  waiting for transfers between devices  9.22 us (22%)
  between operations  0.84 us (2%)
    pallas_call x5, Pallas kernels, call(): pl.pallas_call(kernel, out_shape=outs, in_specs=[pl.BlockSpec(memory_spac...  12.6 us
    ppermute x1, starting transfers between devices, per_device(): off = move(off_own, perm=off_pairs)  5.58 us
    ppermute x1, waiting for transfers between devices, per_device(): fold_a = move(fold_a, perm=to_relay)  5.23 us
    ppermute x1, starting transfers between devices, per_device(): fold_a = move(fold_a, perm=from_relay)  4.16 us
    ppermute x1, starting transfers between devices, per_device(): fold_b = move(fold_b, perm=from_relay)  4.05 us
    ppermute x1, waiting for transfers between devices, per_device(): corner_xs = move(corner_xs, perm=xs_pairs)  3.98 us
    ppermute x1, starting transfers between devices, per_device(): zb = move(zb_own, perm=zb_pairs)  1.92 us
    ppermute x1, starting transfers between devices, per_device(): fold_a = move(fold_a, perm=to_relay)  1.29 us
  transfers between devices with their start and end apart: 9, of which 2 were waited for; matrix products, arithmetic and copies ran while one was open for 0% of the time, Pallas kernels for 8%

profile of v2, /device:TPU:224, one launch (start us, length us, event | category | flops | bytes accessed | tf_op | source)
XLA Modules:
  0.0 41.9 jit_solution(8167844859355496427)
XLA Ops:
  0.6 0.1 pad_add_fusion.place
  0.7 4.7 %shard_map.102 = (f32[4,616,128]{2,1,0:T(8,128)S(1)}, f32[616,128]{1,0:T(8,128)S(1)}, f32[10,8,128]{2,1,0:T(8,128)S(1)}, f32[10,8,128]{2,1,0:T(8,128)S(1)}, f32[...) custom-call(s32[2]{0:T(128)S(1)} %pad_add_fusion.place, f32[75,8,128]{2,1,0:T(8,128)} %temp_hbm.1, ...), custom_call_target="tpu_custom_call" | custom-call | flops 99999997952 | bytes 1000 | tf_op jit(solution)/shard_map/pallas_call | solution.py:457
  5.4 0.0 copy-start
  5.5 0.0 copy-start.2
  5.5 0.0 copy-start.8
  5.5 0.1 collective-permute-start
  5.6 5.6 %collective-permute-start.1 = (f32[10,8,128]{2,1,0:T(8,128)S(1)}, f32[10,8,128]{2,1,0:T(8,128)S(1)}, u32[]{:S(2)}, u32[]{:S(2)}) collective-permute-start(f32[10,8,128]{2,1,0:T(8,128)S(1)} %get-tuple-element.18.off_own), channel_id=1, source_target_pairs={{0,240},{1,241},{2,242},{3,243},{4,244},{5,245},{6,246},{7,247},{8... | collective-permute-start | bytes 122888 | tf_op jit(solution)/shard_map/ppermute | solution.py:505
  11.1 0.6 %shard_map.103 = (f32[680,128]{1,0:T(8,128)S(1)}, f32[344,128]{1,0:T(8,128)S(1)}) custom-call(s32[2]{0:T(128)S(1)} %pad_add_fusion.place, f32[4,616,128]{2,1,0:T(8,128)S(1)} %get-tuple-element.19.state, f32[616,128]{1,0:T(8,128)S(1)} %get-tuple-element.20.wet_ref, f32[4,616,128]{2,1,0:T(8,128)S(1)} %get-tuple-element.16.part), custom_call_target="tpu_custom_call" | custom-call | flops 99999997952 | bytes 1000 | tf_op jit(solution)/shard_map/pallas_call | solution.py:457
  11.8 1.3 %collective-permute-start.3 = (f32[344,128]{1,0:T(8,128)S(1)}, f32[344,128]{1,0:T(8,128)S(1)}, u32[]{:S(2)}, u32[]{:S(2)}) collective-permute-start(f32[344,128]{1,0:T(8,128)S(1)} %get-tuple-element.23), channel_id=1, source_target_pairs={{15,254},{31,238},{47,222},{63,206},{79,190},{95,174},{111,158},{1... | collective-permute-start | bytes 528392 | tf_op jit(solution)/shard_map/ppermute | solution.py:512
  13.1 0.7 %collective-permute-start.2 = (f32[680,128]{1,0:T(8,128)S(1)}, f32[680,128]{1,0:T(8,128)S(1)}, u32[]{:S(2)}, u32[]{:S(2)}) collective-permute-start(f32[680,128]{1,0:T(8,128)S(1)} %get-tuple-element.21.xs_own), channel_id=1, source_target_pairs={{0,1},{1,0},{2,3},{3,2},{4,5},{5,4},{6,7},{7,6},{8,9},{9,8},{10,11... | collective-permute-start | bytes 1044488 | tf_op jit(solution)/shard_map/ppermute | solution.py:513
  13.8 0.0 collective-permute-done.on
  13.8 0.0 copy-start.4
  13.8 0.0 collective-permute-done.1.off
  13.8 0.0 copy-done
  13.8 0.0 copy-done.2
  13.9 0.0 copy-done.8
  13.9 0.0 copy-start.6
  13.9 1.5 %shard_map.104 = (f32[704,128]{1,0:T(8,128)}, f32[360,128]{1,0:T(8,128)S(1)}, f32[24,128]{1,0:T(8,128)}, f32[8,8,128]{2,1,0:T(8,128)S(1)}) custom-call(s32[2]{0:T(128)S(1)} %pad_add_fusion.place, f32[10,8,128]{2,1,0:T(8,128)S(1)} %get-tuple-element.17.on_own, f32[10,8,128]{2,1,0:T(8,128)S(1)} %get-tuple-element.18.off_own, ...), custom_call_target="tpu_custom_call" | custom-call | flops 99999997952 | bytes 1000 | tf_op jit(solution)/shard_map/pallas_call | solution.py:457
  15.4 0.0 copy-done.4
  15.4 0.0 copy-done.6
  15.4 1.3 %collective-permute-start.6 = (f32[360,128]{1,0:T(8,128)S(1)}, f32[360,128]{1,0:T(8,128)}, u32[]{:S(2)}, u32[]{:S(2)}) collective-permute-start(f32[360,128]{1,0:T(8,128)S(1)} %get-tuple-element.26), channel_id=1, source_target_pairs={{15,254},{31,238},{47,222},{63,206},{79,190},{95,174},{111,158},{1... | collective-permute-start | bytes 552968 | tf_op jit(solution)/shard_map/ppermute | solution.py:520
  16.7 5.2 %collective-permute-done.3 = f32[344,128]{1,0:T(8,128)S(1)} collective-permute-done((f32[344,128]{1,0:T(8,128)S(1)}, f32[344,128]{1,0:T(8,128)S(1)}, u32[]{:S(2)}, u32[]{:S(2)}) %collective-permute-start.3) | collective-permute-done | bytes 176160 | tf_op jit(solution)/shard_map/ppermute | solution.py:512
  21.9 4.2 %collective-permute-start.4 = (f32[344,128]{1,0:T(8,128)S(1)}, f32[344,128]{1,0:T(8,128)S(1)}, u32[]{:S(2)}, u32[]{:S(2)}) collective-permute-start(f32[344,128]{1,0:T(8,128)S(1)} %collective-permute-done.3), channel_id=1, source_target_pairs={{14,15},{30,31},{46,47},{62,63},{78,79},{94,95},{110,111},{126,127... | collective-permute-start | bytes 528392 | tf_op jit(solution)/shard_map/ppermute | solution.py:523
  26.1 0.1 collective-permute-start.8
  26.2 1.9 %collective-permute-start.5 = (f32[704,128]{1,0:T(8,128)}, f32[704,128]{1,0:T(8,128)}, u32[]{:S(2)}, u32[]{:S(2)}) collective-permute-start(f32[704,128]{1,0:T(8,128)} %get-tuple-element.25.zb_own), channel_id=1, source_target_pairs={{1,2},{2,1},{3,4},{4,3},{5,6},{6,5},{7,8},{8,7},{9,10},{10,9},{11,... | collective-permute-start | bytes 1081352 | tf_op jit(solution)/shard_map/ppermute | solution.py:521
  28.1 0.0 collective-permute-done.6
  28.1 4.1 %collective-permute-start.7 = (f32[360,128]{1,0:T(8,128)}, f32[360,128]{1,0:T(8,128)}, u32[]{:S(2)}, u32[]{:S(2)}) collective-permute-start(f32[360,128]{1,0:T(8,128)} %collective-permute-done.6), channel_id=1, source_target_pairs={{14,15},{30,31},{46,47},{62,63},{78,79},{94,95},{110,111},{126,127... | collective-permute-start | bytes 552968 | tf_op jit(solution)/shard_map/ppermute | solution.py:524
  32.2 0.0 collective-permute-done.2.xs
  32.2 0.0 collective-permute-done.4.fold_a
  32.2 0.0 copy-start.1
  32.2 0.0 copy-start.3
  32.2 0.0 copy-start.5
  32.2 0.0 copy-start.7
  32.2 0.0 copy-start.9
  32.2 1.2 %shard_map.105.full_in = f32[4,616,128]{2,1,0:T(8,128)S(1)} custom-call(s32[2]{0:T(128)S(1)} %pad_add_fusion.place, f32[4,616,128]{2,1,0:T(8,128)S(1)} %get-tuple-element.16.part, f32[8,8,128]{2,1,0:T(8,128)S(1)} %get-tuple-element.22.extra, f32[680,128]{1,0:T(8,128)S(1)} %collective-permute-done.2.xs, f32[344,128]{1,0:T(8,128)S(1)} %collective-permute-done.4.fold_a), custom_call_target="tpu_custom_call" | custom-call | flops 999999995904 | bytes 1000 | tf_op jit(solution)/shard_map/pallas_call | solution.py:457
  33.4 4.0 %collective-permute-done.8.corner_xs = f32[24,128]{1,0:T(8,128)} collective-permute-done((f32[24,128]{1,0:T(8,128)}, f32[24,128]{1,0:T(8,128)}, u32[]{:S(2)}, u32[]{:S(2)}) %collective-permute-start.8) | collective-permute-done | bytes 12320 | tf_op jit(solution)/shard_map/ppermute | solution.py:522
  37.4 0.0 collective-permute-done.5.zb
  37.4 0.0 collective-permute-done.7.fold_b
  37.4 0.0 copy-done.1
  37.4 0.0 copy-done.3
  37.4 0.0 copy-done.5
  37.4 0.0 copy-done.7
  37.4 0.0 copy-done.9
  37.4 4.5 %shard_map.106 = (f32[75,8,128]{2,1,0:T(8,128)}, f32[75,8,128]{2,1,0:T(8,128)}, f32[75,8,128]{2,1,0:T(8,128)}, f32[75,8,128]{2,1,0:T(8,128)}) custom-call(s32[2]{0:T(128)S(1)} %pad_add_fusion.place, f32[4,616,128]{2,1,0:T(8,128)S(1)} %shard_map.105.full_in, f32[616,128]{1,0:T(8,128)S(1)} %copy-done.9, f32[2,8,128]{2,1,0:T(8,128)S(1)} %get-tuple-element.24.columns_in, ...), custom_call_target="tpu_custom_call" | custom-call | flops 99999997952 | bytes 1000 | tf_op jit(solution)/shard_map/pallas_call | solution.py:457
Async XLA Ops:
  5.4 8.4 %copy-start = (f32[10,8,128]{2,1,0:T(8,128)}, f32[10,8,128]{2,1,0:T(8,128)S(1)}, u32[]{:S(2)}) copy-start(f32[10,8,128]{2,1,0:T(8,128)S(1)} %get-tuple-element.17.on_own) | copy-start | bytes 122884
  5.5 8.4 %copy-start.2 = (f32[10,8,128]{2,1,0:T(8,128)}, f32[10,8,128]{2,1,0:T(8,128)S(1)}, u32[]{:S(2)}) copy-start(f32[10,8,128]{2,1,0:T(8,128)S(1)} %get-tuple-element.18.off_own) | copy-start | bytes 122884
  5.5 8.4 %copy-start.8 = (f32[616,128]{1,0:T(8,128)}, f32[616,128]{1,0:T(8,128)S(1)}, u32[]{:S(2)}) copy-start(f32[616,128]{1,0:T(8,128)S(1)} %get-tuple-element.20.wet_ref) | copy-start | bytes 946180
  5.5 8.4 %collective-permute-start = (f32[10,8,128]{2,1,0:T(8,128)S(1)}, f32[10,8,128]{2,1,0:T(8,128)S(1)}, u32[]{:S(2)}, u32[]{:S(2)}) collective-permute-start(f32[10,8,128]{2,1,0:T(8,128)S(1)} %get-tuple-element.17.on_own), channel_id=1, source_target_pairs={{0,16},{1,17},{2,18},{3,19},{4,20},{5,21},{6,22},{7,23},{8,24},{9,... | collective-permute-start | bytes 122888 | tf_op jit(solution)/shard_map/ppermute | solution.py:504
  5.6 8.3 %collective-permute-start.1 = (f32[10,8,128]{2,1,0:T(8,128)S(1)}, f32[10,8,128]{2,1,0:T(8,128)S(1)}, u32[]{:S(2)}, u32[]{:S(2)}) collective-permute-start(f32[10,8,128]{2,1,0:T(8,128)S(1)} %get-tuple-element.18.off_own), channel_id=1, source_target_pairs={{0,240},{1,241},{2,242},{3,243},{4,244},{5,245},{6,246},{7,247},{8... | collective-permute-start | bytes 122888 | tf_op jit(solution)/shard_map/ppermute | solution.py:505
  11.8 10.1 %collective-permute-start.3 = (f32[344,128]{1,0:T(8,128)S(1)}, f32[344,128]{1,0:T(8,128)S(1)}, u32[]{:S(2)}, u32[]{:S(2)}) collective-permute-start(f32[344,128]{1,0:T(8,128)S(1)} %get-tuple-element.23), channel_id=1, source_target_pairs={{15,254},{31,238},{47,222},{63,206},{79,190},{95,174},{111,158},{1... | collective-permute-start | bytes 528392 | tf_op jit(solution)/shard_map/ppermute | solution.py:512
  13.1 19.1 %collective-permute-start.2 = (f32[680,128]{1,0:T(8,128)S(1)}, f32[680,128]{1,0:T(8,128)S(1)}, u32[]{:S(2)}, u32[]{:S(2)}) collective-permute-start(f32[680,128]{1,0:T(8,128)S(1)} %get-tuple-element.21.xs_own), channel_id=1, source_target_pairs={{0,1},{1,0},{2,3},{3,2},{4,5},{5,4},{6,7},{7,6},{8,9},{9,8},{10,11... | collective-permute-start | bytes 1044488 | tf_op jit(solution)/shard_map/ppermute | solution.py:513
  13.8 1.5 %copy-start.4 = (f32[10,8,128]{2,1,0:T(8,128)}, f32[10,8,128]{2,1,0:T(8,128)S(1)}, u32[]{:S(2)}) copy-start(f32[10,8,128]{2,1,0:T(8,128)S(1)} %collective-permute-done.on) | copy-start | bytes 122884
  13.9 1.5 %copy-start.6 = (f32[10,8,128]{2,1,0:T(8,128)}, f32[10,8,128]{2,1,0:T(8,128)S(1)}, u32[]{:S(2)}) copy-start(f32[10,8,128]{2,1,0:T(8,128)S(1)} %collective-permute-done.1.off) | copy-start | bytes 122884
  15.4 12.7 %collective-permute-start.6 = (f32[360,128]{1,0:T(8,128)S(1)}, f32[360,128]{1,0:T(8,128)}, u32[]{:S(2)}, u32[]{:S(2)}) collective-permute-start(f32[360,128]{1,0:T(8,128)S(1)} %get-tuple-element.26), channel_id=1, source_target_pairs={{15,254},{31,238},{47,222},{63,206},{79,190},{95,174},{111,158},{1... | collective-permute-start | bytes 552968 | tf_op jit(solution)/shard_map/ppermute | solution.py:520
  21.9 10.3 %collective-permute-start.4 = (f32[344,128]{1,0:T(8,128)S(1)}, f32[344,128]{1,0:T(8,128)S(1)}, u32[]{:S(2)}, u32[]{:S(2)}) collective-permute-start(f32[344,128]{1,0:T(8,128)S(1)} %collective-permute-done.3), channel_id=1, source_target_pairs={{14,15},{30,31},{46,47},{62,63},{78,79},{94,95},{110,111},{126,127... | collective-permute-start | bytes 528392 | tf_op jit(solution)/shard_map/ppermute | solution.py:523
  26.1 11.3 %collective-permute-start.8 = (f32[24,128]{1,0:T(8,128)}, f32[24,128]{1,0:T(8,128)}, u32[]{:S(2)}, u32[]{:S(2)}) collective-permute-start(f32[24,128]{1,0:T(8,128)} %get-tuple-element.27), channel_id=1, source_target_pairs={{0,1},{1,0},{2,3},{3,2},{4,5},{5,4},{6,7},{7,6},{8,9},{9,8},{10,11... | collective-permute-start | bytes 36872 | tf_op jit(solution)/shard_map/ppermute | solution.py:522
  26.2 11.2 %collective-permute-start.5 = (f32[704,128]{1,0:T(8,128)}, f32[704,128]{1,0:T(8,128)}, u32[]{:S(2)}, u32[]{:S(2)}) collective-permute-start(f32[704,128]{1,0:T(8,128)} %get-tuple-element.25.zb_own), channel_id=1, source_target_pairs={{1,2},{2,1},{3,4},{4,3},{5,6},{6,5},{7,8},{8,7},{9,10},{10,9},{11,... | collective-permute-start | bytes 1081352 | tf_op jit(solution)/shard_map/ppermute | solution.py:521
  28.1 9.3 %collective-permute-start.7 = (f32[360,128]{1,0:T(8,128)}, f32[360,128]{1,0:T(8,128)}, u32[]{:S(2)}, u32[]{:S(2)}) collective-permute-start(f32[360,128]{1,0:T(8,128)} %collective-permute-done.6), channel_id=1, source_target_pairs={{14,15},{30,31},{46,47},{62,63},{78,79},{94,95},{110,111},{126,127... | collective-permute-start | bytes 552968 | tf_op jit(solution)/shard_map/ppermute | solution.py:524
  32.2 5.2 %copy-start.1 = (f32[10,8,128]{2,1,0:T(8,128)S(1)}, f32[10,8,128]{2,1,0:T(8,128)}, u32[]{:S(2)}) copy-start(f32[10,8,128]{2,1,0:T(8,128)} %copy-done) | copy-start | bytes 122884
  32.2 5.2 %copy-start.3 = (f32[10,8,128]{2,1,0:T(8,128)S(1)}, f32[10,8,128]{2,1,0:T(8,128)}, u32[]{:S(2)}) copy-start(f32[10,8,128]{2,1,0:T(8,128)} %copy-done.2) | copy-start | bytes 122884
  32.2 5.2 %copy-start.5 = (f32[10,8,128]{2,1,0:T(8,128)S(1)}, f32[10,8,128]{2,1,0:T(8,128)}, u32[]{:S(2)}) copy-start(f32[10,8,128]{2,1,0:T(8,128)} %copy-done.4) | copy-start | bytes 122884
  32.2 5.2 %copy-start.7 = (f32[10,8,128]{2,1,0:T(8,128)S(1)}, f32[10,8,128]{2,1,0:T(8,128)}, u32[]{:S(2)}) copy-start(f32[10,8,128]{2,1,0:T(8,128)} %copy-done.6) | copy-start | bytes 122884
  32.2 5.2 %copy-start.9 = (f32[616,128]{1,0:T(8,128)S(1)}, f32[616,128]{1,0:T(8,128)}, u32[]{:S(2)}) copy-start(f32[616,128]{1,0:T(8,128)} %copy-done.8) | copy-start | bytes 946180

commit v3 on v2

--- a/solution.py
+++ b/solution.py
@@ -22,7 +22,8 @@
 PART = 344
 W_ROWS = 10**11
 W_CORNER = 10**11
-W_ADD = 10**12
+W_ADD = 10**11
+W_CHOOSE = 10**12
 
 
 def levels_loop(first, last, unroll, body, carry):
@@ -281,7 +282,7 @@
         fold_b[...] = zb[pl.ds(PART, zb.shape[0] - PART), :]
 
 
-def second_kernel(levels, place, part, extra, xs, fold_a, full):
+def second_kernel(levels, place, part, extra, full):
     _, lane = iotas()
     ends = (lane == 0) | (lane == 127)
 
@@ -300,8 +301,16 @@
             full[i, pl.ds(8 * (edge + 1), 8), :] = zero
 
 
+def choose_kernel(levels, count, place, zb, corner_xs, *refs):
+    corners = refs[count]
+    odd = place[1] % 2 == 1
+    at_end = pl.ds(long_of(levels), 24)
+    corners[pl.ds(0, 24), :] = jnp.where(odd, corner_xs[...], zb[at_end, :])
+    corners[pl.ds(24, 24), :] = jnp.where(odd, zb[at_end, :], corner_xs[...])
+
+
 def third_kernel(levels, tops, place, full_in, wet_ref, columns_in, xs_own, zb_own, xs, zb, fold_a, fold_b,
-                 on_own, off_own, on, off, corner_xs,
+                 on_own, off_own, on, off, corners,
                  temp_hbm, salt_hbm, east_hbm, north_hbm, full, halo, flipped, turned, outs, sems):
     lon_odd = place[0] % 2
     lat_odd = place[1] % 2
@@ -311,9 +320,8 @@
     bat, cor = columns_in[0], columns_in[1]
     full[...] = full_in[...]
 
-    at_end = pl.ds(long_of(levels), 24)
-    south_c = jnp.where(odd, corner_xs[...], zb[at_end, :])
-    north_c = jnp.where(odd, jnp.where(top, fold_b[pl.ds(long_of(levels) - PART, 24), :], zb[at_end, :]), corner_xs[...])
+    south_c = corners[pl.ds(0, 24), :]
+    north_c = jnp.where(top, fold_b[pl.ds(long_of(levels) - PART, 24), :], corners[pl.ds(24, 24), :])
     r = lax.broadcasted_iota(jnp.int32, (24, 128), 0)
     swapped = swap(jnp.concatenate([north_c[10:20], north_c[0:10], north_c[20:24]], axis=0))
     s = r % 10
@@ -454,10 +462,11 @@
 def call(kernel, outs, ins, scratch=(), far_ins=(), far_outs=False, work=10**11):
     vmem = pl.BlockSpec(memory_space=pltpu.VMEM)
     hbm = pl.BlockSpec(memory_space=pltpu.HBM)
+    anywhere = pl.BlockSpec(memory_space=pl.ANY)
     return pl.pallas_call(
         kernel,
         out_shape=outs,
-        in_specs=[pl.BlockSpec(memory_space=pltpu.SMEM)] + [hbm if i in far_ins else vmem for i in range(1, len(ins))],
+        in_specs=[pl.BlockSpec(memory_space=pltpu.SMEM)] + [anywhere if i in far_ins else vmem for i in range(1, len(ins))],
         out_specs=[hbm if far_outs else vmem] * len(outs),
         scratch_shapes=list(scratch),
         compiler_params=pltpu.CompilerParams(vmem_limit_bytes=20 * 2**20),
@@ -522,14 +531,21 @@
     corner_xs = move(corner_xs, perm=xs_pairs)
     fold_a = move(fold_a, perm=from_relay)
     fold_b = move(fold_b, perm=from_relay)
-    full, = call(functools.partial(second_kernel, levels), [shape(4, tall, 128)], [place, part, extra, xs, fold_a], work=W_ADD)
+    full, = call(functools.partial(second_kernel, levels), [shape(4, tall, 128)], [place, part, extra], work=W_ADD)
+    corners, = call(
+        functools.partial(choose_kernel, levels, 2),
+        [shape(48, 128)],
+        [place, zb, corner_xs, xs, fold_a],
+        far_ins=(3, 4),
+        work=W_CHOOSE,
+    )
     out = shape(levels, 8, 128)
     return tuple(
         call(
             functools.partial(third_kernel, levels, count_lat - 1),
             [out] * 4,
             [place, full, wet, columns, xs_own, zb_own, xs, zb, fold_a, fold_b, on_own, off_own, on, off,
-             corner_xs],
+             corners],
             [
                 pltpu.VMEM((4, tall, 128), jnp.float32),
                 pltpu.VMEM((2, 6, 8 * ((levels + 7) // 8), 128), jnp.float32),

time: 42.2 us -> 40.3 us (0.955)
  the two profiles are of different devices: /device:TPU:224 before, /device:TPU:226 now
where the time goes in v3:
time: 40.3 us; the launch traced here: 40 us
  starting transfers between devices  18.3 us (45%)
  Pallas kernels  13.7 us (34%)
  waiting for transfers between devices  7 us (17%)
  between operations  0.83 us (2%)
    pallas_call x6, Pallas kernels, call(): pl.pallas_call(kernel, out_shape=outs, in_specs=[pl.BlockSpec(memory_spac...  13.7 us
    ppermute x1, starting transfers between devices, per_device(): fold_b = move(fold_b, perm=to_relay)  6.75 us
    ppermute x1, starting transfers between devices, per_device(): off = move(off_own, perm=off_pairs)  4.68 us
    ppermute x1, waiting for transfers between devices, per_device(): fold_b = move(fold_b, perm=from_relay)  3.02 us
    ppermute x1, waiting for transfers between devices, per_device(): corner_xs = move(corner_xs, perm=xs_pairs)  2.01 us
    ppermute x1, waiting for transfers between devices, per_device(): fold_a = move(fold_a, perm=from_relay)  1.95 us
    ppermute x1, starting transfers between devices, per_device(): xs = move(xs_own, perm=xs_pairs)  1.47 us
    ppermute x1, starting transfers between devices, per_device(): fold_b = move(fold_b, perm=from_relay)  1.29 us
  transfers between devices with their start and end apart: 9, of which 3 were waited for; matrix products, arithmetic and copies ran while one was open for 0% of the time, Pallas kernels for 11%

profile of v3, /device:TPU:226, one launch (start us, length us, event | category | flops | bytes accessed | tf_op | source)
XLA Modules:
  0.0 40.0 jit_solution(7674587341951521372)
XLA Ops:
  0.6 0.1 pad_add_fusion.place
  0.7 4.7 %shard_map.102 = (f32[4,616,128]{2,1,0:T(8,128)S(1)}, f32[616,128]{1,0:T(8,128)S(1)}, f32[10,8,128]{2,1,0:T(8,128)S(1)}, f32[10,8,128]{2,1,0:T(8,128)S(1)}, f32[...) custom-call(s32[2]{0:T(128)S(1)} %pad_add_fusion.place, f32[75,8,128]{2,1,0:T(8,128)} %temp_hbm.1, ...), custom_call_target="tpu_custom_call" | custom-call | flops 99999997952 | bytes 1000 | tf_op jit(solution)/shard_map/pallas_call | solution.py:466
  5.4 0.0 copy-start.2
  5.5 0.0 copy-start.4
  5.5 0.0 copy-start.8
  5.5 0.1 collective-permute-start
  5.6 4.7 %collective-permute-start.1 = (f32[10,8,128]{2,1,0:T(8,128)S(1)}, f32[10,8,128]{2,1,0:T(8,128)S(1)}, u32[]{:S(2)}, u32[]{:S(2)}) collective-permute-start(f32[10,8,128]{2,1,0:T(8,128)S(1)} %get-tuple-element.18.off_own), channel_id=1, source_target_pairs={{0,240},{1,241},{2,242},{3,243},{4,244},{5,245},{6,246},{7,247},{8... | collective-permute-start | bytes 122888 | tf_op jit(solution)/shard_map/ppermute | solution.py:514
  10.3 1.4 %shard_map.103 = (f32[680,128]{1,0:T(8,128)}, f32[344,128]{1,0:T(8,128)S(1)}) custom-call(s32[2]{0:T(128)S(1)} %pad_add_fusion.place, f32[4,616,128]{2,1,0:T(8,128)S(1)} %get-tuple-element.19.state, f32[616,128]{1,0:T(8,128)S(1)} %get-tuple-element.20.wet_ref, f32[4,616,128]{2,1,0:T(8,128)S(1)} %get-tuple-element.16.part), custom_call_target="tpu_custom_call" | custom-call | flops 99999997952 | bytes 1000 | tf_op jit(solution)/shard_map/pallas_call | solution.py:466
  11.7 1.3 %collective-permute-start.4 = (f32[344,128]{1,0:T(8,128)S(1)}, f32[344,128]{1,0:T(8,128)S(1)}, u32[]{:S(2)}, u32[]{:S(2)}) collective-permute-start(f32[344,128]{1,0:T(8,128)S(1)} %get-tuple-element.25), channel_id=1, source_target_pairs={{15,254},{31,238},{47,222},{63,206},{79,190},{95,174},{111,158},{1... | collective-permute-start | bytes 528392 | tf_op jit(solution)/shard_map/ppermute | solution.py:521
  13.0 1.5 %collective-permute-start.2 = (f32[680,128]{1,0:T(8,128)}, f32[680,128]{1,0:T(8,128)}, u32[]{:S(2)}, u32[]{:S(2)}) collective-permute-start(f32[680,128]{1,0:T(8,128)} %get-tuple-element.21.xs_own), channel_id=1, source_target_pairs={{0,1},{1,0},{2,3},{3,2},{4,5},{5,4},{6,7},{7,6},{8,9},{9,8},{10,11... | collective-permute-start | bytes 1044488 | tf_op jit(solution)/shard_map/ppermute | solution.py:522
  14.4 0.0 collective-permute-done.on
  14.4 0.0 copy-start.6
  14.4 0.0 collective-permute-done.1.off
  14.4 0.0 copy-done.2
  14.5 0.0 copy-done.4
  14.5 0.0 copy-done.8
  14.5 1.2 %shard_map.104 = (f32[704,128]{1,0:T(8,128)S(1)}, f32[360,128]{1,0:T(8,128)S(1)}, f32[24,128]{1,0:T(8,128)S(1)}, f32[8,8,128]{2,1,0:T(8,128)S(1)}) custom-call(s32[2]{0:T(128)S(1)} %pad_add_fusion.place, f32[10,8,128]{2,1,0:T(8,128)S(1)} %get-tuple-element.17.on_own, f32[10,8,128]{2,1,0:T(8,128)S(1)} %get-tuple-element.18.off_own, ...), custom_call_target="tpu_custom_call" | custom-call | flops 99999997952 | bytes 1000 | tf_op jit(solution)/shard_map/pallas_call | solution.py:466
  15.7 0.0 copy-done.6
  15.7 0.0 copy-start
  15.7 0.7 %collective-permute-start.8 = (f32[24,128]{1,0:T(8,128)S(1)}, f32[24,128]{1,0:T(8,128)S(1)}, u32[]{:S(2)}, u32[]{:S(2)}) collective-permute-start(f32[24,128]{1,0:T(8,128)S(1)} %get-tuple-element.27), channel_id=1, source_target_pairs={{0,1},{1,0},{2,3},{3,2},{4,5},{5,4},{6,7},{7,6},{8,9},{9,8},{10,11... | collective-permute-start | bytes 36872 | tf_op jit(solution)/shard_map/ppermute | solution.py:531
  16.4 6.7 %collective-permute-start.6 = (f32[360,128]{1,0:T(8,128)S(1)}, f32[360,128]{1,0:T(8,128)}, u32[]{:S(2)}, u32[]{:S(2)}) collective-permute-start(f32[360,128]{1,0:T(8,128)S(1)} %get-tuple-element.26), channel_id=1, source_target_pairs={{15,254},{31,238},{47,222},{63,206},{79,190},{95,174},{111,158},{1... | collective-permute-start | bytes 552968 | tf_op jit(solution)/shard_map/ppermute | solution.py:529
  23.2 0.7 %collective-permute-start.3 = (f32[704,128]{1,0:T(8,128)S(1)}, f32[704,128]{1,0:T(8,128)S(1)}, u32[]{:S(2)}, u32[]{:S(2)}) collective-permute-start(f32[704,128]{1,0:T(8,128)S(1)} %get-tuple-element.24.zb_own), channel_id=1, source_target_pairs={{1,2},{2,1},{3,4},{4,3},{5,6},{6,5},{7,8},{8,7},{9,10},{10,9},{11,... | collective-permute-start | bytes 1081352 | tf_op jit(solution)/shard_map/ppermute | solution.py:530
  23.8 0.0 collective-permute-done.4
  23.9 1.3 %collective-permute-start.5 = (f32[344,128]{1,0:T(8,128)S(1)}, f32[344,128]{1,0:T(8,128)S(1)}, u32[]{:S(2)}, u32[]{:S(2)}) collective-permute-start(f32[344,128]{1,0:T(8,128)S(1)} %collective-permute-done.4), channel_id=1, source_target_pairs={{14,15},{30,31},{46,47},{62,63},{78,79},{94,95},{110,111},{126,127... | collective-permute-start | bytes 528392 | tf_op jit(solution)/shard_map/ppermute | solution.py:532
  25.2 1.2 %shard_map.105.full_in = f32[4,616,128]{2,1,0:T(8,128)S(1)} custom-call(s32[2]{0:T(128)S(1)} %pad_add_fusion.place, f32[4,616,128]{2,1,0:T(8,128)S(1)} %get-tuple-element.16.part, f32[8,8,128]{2,1,0:T(8,128)S(1)} %get-tuple-element.22.extra), custom_call_target="tpu_custom_call" | custom-call | flops 99999997952 | bytes 1000 | tf_op jit(solution)/shard_map/pallas_call | solution.py:466
  26.3 0.0 copy-done
  26.3 0.0 collective-permute-done.6
  26.4 1.3 %collective-permute-start.7 = (f32[360,128]{1,0:T(8,128)}, f32[360,128]{1,0:T(8,128)}, u32[]{:S(2)}, u32[]{:S(2)}) collective-permute-start(f32[360,128]{1,0:T(8,128)} %collective-permute-done.6), channel_id=1, source_target_pairs={{14,15},{30,31},{46,47},{62,63},{78,79},{94,95},{110,111},{126,127... | collective-permute-start | bytes 552968 | tf_op jit(solution)/shard_map/ppermute | solution.py:533
  27.7 2.0 %collective-permute-done.8.corner_xs = f32[24,128]{1,0:T(8,128)S(1)} collective-permute-done((f32[24,128]{1,0:T(8,128)S(1)}, f32[24,128]{1,0:T(8,128)S(1)}, u32[]{:S(2)}, u32[]{:S(2)}) %collective-permute-start.8) | collective-permute-done | bytes 12320 | tf_op jit(solution)/shard_map/ppermute | solution.py:531
  29.7 0.0 collective-permute-done.2.refs_0_.xs
  29.7 2.0 %collective-permute-done.5.refs_1_.fold_a = f32[344,128]{1,0:T(8,128)S(1)} collective-permute-done((f32[344,128]{1,0:T(8,128)S(1)}, f32[344,128]{1,0:T(8,128)S(1)}, u32[]{:S(2)}, u32[]{:S(2)}) %collective-permute-start.5) | collective-permute-done | bytes 176160 | tf_op jit(solution)/shard_map/ppermute | solution.py:532
  31.6 0.0 collective-permute-done.3.zb
  31.6 0.0 copy-start.1
  31.6 0.0 copy-start.3
  31.6 0.0 copy-start.5
  31.6 0.0 copy-start.7
  31.7 0.0 copy-start.9
  31.7 0.6 %shard_map.106.corners = f32[48,128]{1,0:T(8,128)S(1)} custom-call(s32[2]{0:T(128)S(1)} %pad_add_fusion.place, f32[704,128]{1,0:T(8,128)S(1)} %collective-permute-done.3.zb, f32[24,128]{1,0:T(8,128)S(1)} %collective-permute-done.8.corner_xs, f32[680,128]{1,0:T(8,128)} %collective-permute-done.2.refs_0_.xs, f32[344,128]{1,0:T(8,128)S(1)} %collective-permute-done.5.refs_1_.fold_a), custom_call_target="tpu_custom_call" | custom-call | flops 999999995904 | bytes 1000 | tf_op jit(solution)/shard_map/pallas_call | solution.py:466
  32.2 3.0 %collective-permute-done.7.fold_b = f32[360,128]{1,0:T(8,128)} collective-permute-done((f32[360,128]{1,0:T(8,128)}, f32[360,128]{1,0:T(8,128)}, u32[]{:S(2)}, u32[]{:S(2)}) %collective-permute-start.7) | collective-permute-done | bytes 184352 | tf_op jit(solution)/shard_map/ppermute | solution.py:533
  35.3 0.0 copy-done.1
  35.3 0.0 copy-done.3
  35.3 0.0 copy-done.5
  35.3 0.0 copy-done.7
  35.3 0.0 copy-done.9
  35.3 4.7 %shard_map.107 = (f32[75,8,128]{2,1,0:T(8,128)}, f32[75,8,128]{2,1,0:T(8,128)}, f32[75,8,128]{2,1,0:T(8,128)}, f32[75,8,128]{2,1,0:T(8,128)}) custom-call(s32[2]{0:T(128)S(1)} %pad_add_fusion.place, f32[4,616,128]{2,1,0:T(8,128)S(1)} %shard_map.105.full_in, f32[616,128]{1,0:T(8,128)S(1)} %copy-done.9, f32[2,8,128]{2,1,0:T(8,128)S(1)} %get-tuple-element.23.columns_in, ...), custom_call_target="tpu_custom_call" | custom-call | flops 99999997952 | bytes 1000 | tf_op jit(solution)/shard_map/pallas_call | solution.py:466
Async XLA Ops:
  5.4 9.0 %copy-start.2 = (f32[10,8,128]{2,1,0:T(8,128)}, f32[10,8,128]{2,1,0:T(8,128)S(1)}, u32[]{:S(2)}) copy-start(f32[10,8,128]{2,1,0:T(8,128)S(1)} %get-tuple-element.17.on_own) | copy-start | bytes 122884
  5.5 9.0 %copy-start.4 = (f32[10,8,128]{2,1,0:T(8,128)}, f32[10,8,128]{2,1,0:T(8,128)S(1)}, u32[]{:S(2)}) copy-start(f32[10,8,128]{2,1,0:T(8,128)S(1)} %get-tuple-element.18.off_own) | copy-start | bytes 122884
  5.5 9.0 %copy-start.8 = (f32[616,128]{1,0:T(8,128)}, f32[616,128]{1,0:T(8,128)S(1)}, u32[]{:S(2)}) copy-start(f32[616,128]{1,0:T(8,128)S(1)} %get-tuple-element.20.wet_ref) | copy-start | bytes 946180
  5.5 9.0 %collective-permute-start = (f32[10,8,128]{2,1,0:T(8,128)S(1)}, f32[10,8,128]{2,1,0:T(8,128)S(1)}, u32[]{:S(2)}, u32[]{:S(2)}) collective-permute-start(f32[10,8,128]{2,1,0:T(8,128)S(1)} %get-tuple-element.17.on_own), channel_id=1, source_target_pairs={{0,16},{1,17},{2,18},{3,19},{4,20},{5,21},{6,22},{7,23},{8,24},{9,... | collective-permute-start | bytes 122888 | tf_op jit(solution)/shard_map/ppermute | solution.py:513
  5.6 8.9 %collective-permute-start.1 = (f32[10,8,128]{2,1,0:T(8,128)S(1)}, f32[10,8,128]{2,1,0:T(8,128)S(1)}, u32[]{:S(2)}, u32[]{:S(2)}) collective-permute-start(f32[10,8,128]{2,1,0:T(8,128)S(1)} %get-tuple-element.18.off_own), channel_id=1, source_target_pairs={{0,240},{1,241},{2,242},{3,243},{4,244},{5,245},{6,246},{7,247},{8... | collective-permute-start | bytes 122888 | tf_op jit(solution)/shard_map/ppermute | solution.py:514
  11.7 12.2 %collective-permute-start.4 = (f32[344,128]{1,0:T(8,128)S(1)}, f32[344,128]{1,0:T(8,128)S(1)}, u32[]{:S(2)}, u32[]{:S(2)}) collective-permute-start(f32[344,128]{1,0:T(8,128)S(1)} %get-tuple-element.25), channel_id=1, source_target_pairs={{15,254},{31,238},{47,222},{63,206},{79,190},{95,174},{111,158},{1... | collective-permute-start | bytes 528392 | tf_op jit(solution)/shard_map/ppermute | solution.py:521
  13.0 16.7 %collective-permute-start.2 = (f32[680,128]{1,0:T(8,128)}, f32[680,128]{1,0:T(8,128)}, u32[]{:S(2)}, u32[]{:S(2)}) collective-permute-start(f32[680,128]{1,0:T(8,128)} %get-tuple-element.21.xs_own), channel_id=1, source_target_pairs={{0,1},{1,0},{2,3},{3,2},{4,5},{5,4},{6,7},{7,6},{8,9},{9,8},{10,11... | collective-permute-start | bytes 1044488 | tf_op jit(solution)/shard_map/ppermute | solution.py:522
  14.4 1.2 %copy-start.6 = (f32[10,8,128]{2,1,0:T(8,128)}, f32[10,8,128]{2,1,0:T(8,128)S(1)}, u32[]{:S(2)}) copy-start(f32[10,8,128]{2,1,0:T(8,128)S(1)} %collective-permute-done.on) | copy-start | bytes 122884
  15.7 10.7 %copy-start = (f32[704,128]{1,0:T(8,128)}, f32[704,128]{1,0:T(8,128)S(1)}, u32[]{:S(2)}) copy-start(f32[704,128]{1,0:T(8,128)S(1)} %get-tuple-element.24.zb_own) | copy-start | bytes 1081348
  15.7 14.0 %collective-permute-start.8 = (f32[24,128]{1,0:T(8,128)S(1)}, f32[24,128]{1,0:T(8,128)S(1)}, u32[]{:S(2)}, u32[]{:S(2)}) collective-permute-start(f32[24,128]{1,0:T(8,128)S(1)} %get-tuple-element.27), channel_id=1, source_target_pairs={{0,1},{1,0},{2,3},{3,2},{4,5},{5,4},{6,7},{7,6},{8,9},{9,8},{10,11... | collective-permute-start | bytes 36872 | tf_op jit(solution)/shard_map/ppermute | solution.py:531
  16.4 9.9 %collective-permute-start.6 = (f32[360,128]{1,0:T(8,128)S(1)}, f32[360,128]{1,0:T(8,128)}, u32[]{:S(2)}, u32[]{:S(2)}) collective-permute-start(f32[360,128]{1,0:T(8,128)S(1)} %get-tuple-element.26), channel_id=1, source_target_pairs={{15,254},{31,238},{47,222},{63,206},{79,190},{95,174},{111,158},{1... | collective-permute-start | bytes 552968 | tf_op jit(solution)/shard_map/ppermute | solution.py:529
  23.2 8.5 %collective-permute-start.3 = (f32[704,128]{1,0:T(8,128)S(1)}, f32[704,128]{1,0:T(8,128)S(1)}, u32[]{:S(2)}, u32[]{:S(2)}) collective-permute-start(f32[704,128]{1,0:T(8,128)S(1)} %get-tuple-element.24.zb_own), channel_id=1, source_target_pairs={{1,2},{2,1},{3,4},{4,3},{5,6},{6,5},{7,8},{8,7},{9,10},{10,9},{11,... | collective-permute-start | bytes 1081352 | tf_op jit(solution)/shard_map/ppermute | solution.py:530
  23.9 7.8 %collective-permute-start.5 = (f32[344,128]{1,0:T(8,128)S(1)}, f32[344,128]{1,0:T(8,128)S(1)}, u32[]{:S(2)}, u32[]{:S(2)}) collective-permute-start(f32[344,128]{1,0:T(8,128)S(1)} %collective-permute-done.4), channel_id=1, source_target_pairs={{14,15},{30,31},{46,47},{62,63},{78,79},{94,95},{110,111},{126,127... | collective-permute-start | bytes 528392 | tf_op jit(solution)/shard_map/ppermute | solution.py:532
  26.4 8.9 %collective-permute-start.7 = (f32[360,128]{1,0:T(8,128)}, f32[360,128]{1,0:T(8,128)}, u32[]{:S(2)}, u32[]{:S(2)}) collective-permute-start(f32[360,128]{1,0:T(8,128)} %collective-permute-done.6), channel_id=1, source_target_pairs={{14,15},{30,31},{46,47},{62,63},{78,79},{94,95},{110,111},{126,127... | collective-permute-start | bytes 552968 | tf_op jit(solution)/shard_map/ppermute | solution.py:533
  31.6 3.6 %copy-start.1 = (f32[704,128]{1,0:T(8,128)S(1)}, f32[704,128]{1,0:T(8,128)}, u32[]{:S(2)}) copy-start(f32[704,128]{1,0:T(8,128)} %copy-done) | copy-start | bytes 1081348
  31.6 3.6 %copy-start.3 = (f32[10,8,128]{2,1,0:T(8,128)S(1)}, f32[10,8,128]{2,1,0:T(8,128)}, u32[]{:S(2)}) copy-start(f32[10,8,128]{2,1,0:T(8,128)} %copy-done.2) | copy-start | bytes 122884
  31.6 3.6 %copy-start.5 = (f32[10,8,128]{2,1,0:T(8,128)S(1)}, f32[10,8,128]{2,1,0:T(8,128)}, u32[]{:S(2)}) copy-start(f32[10,8,128]{2,1,0:T(8,128)} %copy-done.4) | copy-start | bytes 122884
  31.6 3.6 %copy-start.7 = (f32[10,8,128]{2,1,0:T(8,128)S(1)}, f32[10,8,128]{2,1,0:T(8,128)}, u32[]{:S(2)}) copy-start(f32[10,8,128]{2,1,0:T(8,128)} %copy-done.6) | copy-start | bytes 122884
  31.7 3.6 %copy-start.9 = (f32[616,128]{1,0:T(8,128)S(1)}, f32[616,128]{1,0:T(8,128)}, u32[]{:S(2)}) copy-start(f32[616,128]{1,0:T(8,128)} %copy-done.8) | copy-start | bytes 946180

commit v4 on v3

--- a/solution.py
+++ b/solution.py
@@ -15,15 +15,15 @@
 DRAG = 2.0
 HIGH = lax.Precision.HIGHEST
 LOW = 64
-UNROLL_A = 5
-UNROLL_B = 15
+UNROLL_A = 25
+UNROLL_B = 25
 UNROLL_C = 16
 UNROLL_D = 25
 PART = 344
-W_ROWS = 10**11
-W_CORNER = 10**11
-W_ADD = 10**11
-W_CHOOSE = 10**12
+W_ROWS = 2*10**10
+W_CORNER = 2*10**10
+W_ADD = 2*10**10
+W_CHOOSE = 2*10**10
 
 
 def levels_loop(first, last, unroll, body, carry):
@@ -459,7 +459,7 @@
     return jax.ShapeDtypeStruct(dims, jnp.float32)
 
 
-def call(kernel, outs, ins, scratch=(), far_ins=(), far_outs=False, work=10**11):
+def call(kernel, outs, ins, scratch=(), far_ins=(), far_outs=False, work=2*10**10):
     vmem = pl.BlockSpec(memory_space=pltpu.VMEM)
     hbm = pl.BlockSpec(memory_space=pltpu.HBM)
     anywhere = pl.BlockSpec(memory_space=pl.ANY)

time: 40.3 us -> 37.8 us (0.938)
  Pallas kernels: 13.7 us -> 11.9 us
  starting transfers between devices: 18.3 us -> 17.6 us
    pallas_call x6, Pallas kernels: 13.7 us -> 11.9 us  [call(): pl.pallas_call(kernel, out_shape=outs, in_specs=[pl.BlockSpec(memory_spac...]
    ppermute x1, waiting for transfers between devices: 1.95 us -> 0.64 us  [per_device(): fold_a = move(fold_a, perm=from_relay)]
    ppermute x1, waiting for transfers between devices: 2.01 us -> 3 us  [per_device(): corner_xs = move(corner_xs, perm=xs_pairs)]
    ppermute x1, starting transfers between devices: 6.75 us -> 6.1 us  [per_device(): fold_b = move(fold_b, perm=to_relay)]
  transfers between devices with their start and end apart: 9 -> 9, of which waited for: 3 -> 3; matrix products, arithmetic and copies ran while one was open for 0% -> 0% of each run, Pallas kernels for 11% -> 8%
where the time goes in v4:
time: 37.8 us; the launch traced here: 37.2 us
  starting transfers between devices  17.6 us (47%)
  Pallas kernels  11.9 us (31%)
  waiting for transfers between devices  6.94 us (18%)
  between operations  0.73 us (2%)
    pallas_call x6, Pallas kernels, call(): pl.pallas_call(kernel, out_shape=outs, in_specs=[pl.BlockSpec(memory_spac...  11.9 us
    ppermute x1, starting transfers between devices, per_device(): fold_b = move(fold_b, perm=to_relay)  6.1 us
    ppermute x1, starting transfers between devices, per_device(): off = move(off_own, perm=off_pairs)  4.68 us
    ppermute x1, waiting for transfers between devices, per_device(): fold_b = move(fold_b, perm=from_relay)  3.29 us
    ppermute x1, waiting for transfers between devices, per_device(): corner_xs = move(corner_xs, perm=xs_pairs)  3 us
    ppermute x1, starting transfers between devices, per_device(): xs = move(xs_own, perm=xs_pairs)  1.48 us
    ppermute x1, starting transfers between devices, per_device(): fold_a = move(fold_a, perm=to_relay)  1.3 us
    ppermute x1, starting transfers between devices, per_device(): fold_a = move(fold_a, perm=from_relay)  1.29 us
  transfers between devices with their start and end apart: 9, of which 3 were waited for; matrix products, arithmetic and copies ran while one was open for 0% of the time, Pallas kernels for 8%

profile of v4, /device:TPU:226, one launch (start us, length us, event | category | flops | bytes accessed | tf_op | source)
XLA Modules:
  0.0 37.2 jit_solution(9936678547518806286)
XLA Ops:
  0.6 0.1 pad_add_fusion.place
  0.7 4.6 %shard_map.102 = (f32[4,616,128]{2,1,0:T(8,128)S(1)}, f32[616,128]{1,0:T(8,128)S(1)}, f32[10,8,128]{2,1,0:T(8,128)S(1)}, f32[10,8,128]{2,1,0:T(8,128)S(1)}, f32[...) custom-call(s32[2]{0:T(128)S(1)} %pad_add_fusion.place, f32[75,8,128]{2,1,0:T(8,128)} %temp_hbm.1, ...), custom_call_target="tpu_custom_call" | custom-call | flops 20000000000 | bytes 1000 | tf_op jit(solution)/shard_map/pallas_call | solution.py:466
  5.3 0.1 collective-permute-start
  5.4 4.7 %collective-permute-start.1 = (f32[10,8,128]{2,1,0:T(8,128)S(1)}, f32[10,8,128]{2,1,0:T(8,128)S(1)}, u32[]{:S(2)}, u32[]{:S(2)}) collective-permute-start(f32[10,8,128]{2,1,0:T(8,128)S(1)} %get-tuple-element.18.off_own), channel_id=1, source_target_pairs={{0,240},{1,241},{2,242},{3,243},{4,244},{5,245},{6,246},{7,247},{8... | collective-permute-start | bytes 122888 | tf_op jit(solution)/shard_map/ppermute | solution.py:514
  10.1 0.7 %shard_map.103 = (f32[680,128]{1,0:T(8,128)S(1)}, f32[344,128]{1,0:T(8,128)S(1)}) custom-call(s32[2]{0:T(128)S(1)} %pad_add_fusion.place, f32[4,616,128]{2,1,0:T(8,128)S(1)} %get-tuple-element.19.state, f32[616,128]{1,0:T(8,128)S(1)} %get-tuple-element.20.wet_ref, f32[4,616,128]{2,1,0:T(8,128)S(1)} %get-tuple-element.16.part), custom_call_target="tpu_custom_call" | custom-call | flops 20000000000 | bytes 1000 | tf_op jit(solution)/shard_map/pallas_call | solution.py:466
  10.8 1.3 %collective-permute-start.4 = (f32[344,128]{1,0:T(8,128)S(1)}, f32[344,128]{1,0:T(8,128)S(1)}, u32[]{:S(2)}, u32[]{:S(2)}) collective-permute-start(f32[344,128]{1,0:T(8,128)S(1)} %get-tuple-element.25), channel_id=1, source_target_pairs={{15,254},{31,238},{47,222},{63,206},{79,190},{95,174},{111,158},{1... | collective-permute-start | bytes 528392 | tf_op jit(solution)/shard_map/ppermute | solution.py:521
  12.1 1.5 %collective-permute-start.2 = (f32[680,128]{1,0:T(8,128)S(1)}, f32[680,128]{1,0:T(8,128)S(1)}, u32[]{:S(2)}, u32[]{:S(2)}) collective-permute-start(f32[680,128]{1,0:T(8,128)S(1)} %get-tuple-element.21.xs_own), channel_id=1, source_target_pairs={{0,1},{1,0},{2,3},{3,2},{4,5},{5,4},{6,7},{7,6},{8,9},{9,8},{10,11... | collective-permute-start | bytes 1044488 | tf_op jit(solution)/shard_map/ppermute | solution.py:522
  13.6 0.0 collective-permute-done.on
  13.6 0.0 collective-permute-done.1.off
  13.6 0.7 %shard_map.104 = (f32[704,128]{1,0:T(8,128)S(1)}, f32[360,128]{1,0:T(8,128)S(1)}, f32[24,128]{1,0:T(8,128)S(1)}, f32[8,8,128]{2,1,0:T(8,128)S(1)}) custom-call(s32[2]{0:T(128)S(1)} %pad_add_fusion.place, f32[10,8,128]{2,1,0:T(8,128)S(1)} %get-tuple-element.17.on_own, f32[10,8,128]{2,1,0:T(8,128)S(1)} %get-tuple-element.18.off_own, ...), custom_call_target="tpu_custom_call" | custom-call | flops 20000000000 | bytes 1000 | tf_op jit(solution)/shard_map/pallas_call | solution.py:466
  14.3 0.7 %collective-permute-start.8 = (f32[24,128]{1,0:T(8,128)S(1)}, f32[24,128]{1,0:T(8,128)S(1)}, u32[]{:S(2)}, u32[]{:S(2)}) collective-permute-start(f32[24,128]{1,0:T(8,128)S(1)} %get-tuple-element.27), channel_id=1, source_target_pairs={{0,1},{1,0},{2,3},{3,2},{4,5},{5,4},{6,7},{7,6},{8,9},{9,8},{10,11... | collective-permute-start | bytes 36872 | tf_op jit(solution)/shard_map/ppermute | solution.py:531
  15.0 6.1 %collective-permute-start.6 = (f32[360,128]{1,0:T(8,128)S(1)}, f32[360,128]{1,0:T(8,128)S(1)}, u32[]{:S(2)}, u32[]{:S(2)}) collective-permute-start(f32[360,128]{1,0:T(8,128)S(1)} %get-tuple-element.26), channel_id=1, source_target_pairs={{15,254},{31,238},{47,222},{63,206},{79,190},{95,174},{111,158},{1... | collective-permute-start | bytes 552968 | tf_op jit(solution)/shard_map/ppermute | solution.py:529
  21.1 0.7 %collective-permute-start.3 = (f32[704,128]{1,0:T(8,128)S(1)}, f32[704,128]{1,0:T(8,128)S(1)}, u32[]{:S(2)}, u32[]{:S(2)}) collective-permute-start(f32[704,128]{1,0:T(8,128)S(1)} %get-tuple-element.24.zb_own), channel_id=1, source_target_pairs={{1,2},{2,1},{3,4},{4,3},{5,6},{6,5},{7,8},{8,7},{9,10},{10,9},{11,... | collective-permute-start | bytes 1081352 | tf_op jit(solution)/shard_map/ppermute | solution.py:530
  21.8 0.0 collective-permute-done.4
  21.8 1.3 %collective-permute-start.5 = (f32[344,128]{1,0:T(8,128)S(1)}, f32[344,128]{1,0:T(8,128)S(1)}, u32[]{:S(2)}, u32[]{:S(2)}) collective-permute-start(f32[344,128]{1,0:T(8,128)S(1)} %collective-permute-done.4), channel_id=1, source_target_pairs={{14,15},{30,31},{46,47},{62,63},{78,79},{94,95},{110,111},{126,127... | collective-permute-start | bytes 528392 | tf_op jit(solution)/shard_map/ppermute | solution.py:532
  23.1 1.2 %shard_map.105.full_in = f32[4,616,128]{2,1,0:T(8,128)S(1)} custom-call(s32[2]{0:T(128)S(1)} %pad_add_fusion.place, f32[4,616,128]{2,1,0:T(8,128)S(1)} %get-tuple-element.16.part, f32[8,8,128]{2,1,0:T(8,128)S(1)} %get-tuple-element.22.extra), custom_call_target="tpu_custom_call" | custom-call | flops 20000000000 | bytes 1000 | tf_op jit(solution)/shard_map/pallas_call | solution.py:466
  24.3 0.0 collective-permute-done.6
  24.3 1.3 %collective-permute-start.7 = (f32[360,128]{1,0:T(8,128)S(1)}, f32[360,128]{1,0:T(8,128)S(1)}, u32[]{:S(2)}, u32[]{:S(2)}) collective-permute-start(f32[360,128]{1,0:T(8,128)S(1)} %collective-permute-done.6), channel_id=1, source_target_pairs={{14,15},{30,31},{46,47},{62,63},{78,79},{94,95},{110,111},{126,127... | collective-permute-start | bytes 552968 | tf_op jit(solution)/shard_map/ppermute | solution.py:533
  25.6 3.0 %collective-permute-done.8.corner_xs = f32[24,128]{1,0:T(8,128)S(1)} collective-permute-done((f32[24,128]{1,0:T(8,128)S(1)}, f32[24,128]{1,0:T(8,128)S(1)}, u32[]{:S(2)}, u32[]{:S(2)}) %collective-permute-start.8) | collective-permute-done | bytes 12320 | tf_op jit(solution)/shard_map/ppermute | solution.py:531
  28.6 0.0 collective-permute-done.2.refs_0_.xs
  28.6 0.6 %collective-permute-done.5.refs_1_.fold_a = f32[344,128]{1,0:T(8,128)S(1)} collective-permute-done((f32[344,128]{1,0:T(8,128)S(1)}, f32[344,128]{1,0:T(8,128)S(1)}, u32[]{:S(2)}, u32[]{:S(2)}) %collective-permute-start.5) | collective-permute-done | bytes 176160 | tf_op jit(solution)/shard_map/ppermute | solution.py:532
  29.2 0.0 collective-permute-done.3.zb
  29.2 0.6 %shard_map.106.corners = f32[48,128]{1,0:T(8,128)S(1)} custom-call(s32[2]{0:T(128)S(1)} %pad_add_fusion.place, f32[704,128]{1,0:T(8,128)S(1)} %collective-permute-done.3.zb, f32[24,128]{1,0:T(8,128)S(1)} %collective-permute-done.8.corner_xs, f32[680,128]{1,0:T(8,128)S(1)} %collective-permute-done.2.refs_0_.xs, ...), custom_call_target="tpu_custom_call" | custom-call | flops 20000000000 | bytes 1000 | tf_op jit(solution)/shard_map/pallas_call | solution.py:466
  29.8 3.3 %collective-permute-done.7.fold_b = f32[360,128]{1,0:T(8,128)S(1)} collective-permute-done((f32[360,128]{1,0:T(8,128)S(1)}, f32[360,128]{1,0:T(8,128)S(1)}, u32[]{:S(2)}, u32[]{:S(2)}) %collective-permute-start.7) | collective-permute-done | bytes 184352 | tf_op jit(solution)/shard_map/ppermute | solution.py:533
  33.1 4.1 %shard_map.107 = (f32[75,8,128]{2,1,0:T(8,128)}, f32[75,8,128]{2,1,0:T(8,128)}, f32[75,8,128]{2,1,0:T(8,128)}, f32[75,8,128]{2,1,0:T(8,128)}) custom-call(s32[2]{0:T(128)S(1)} %pad_add_fusion.place, f32[4,616,128]{2,1,0:T(8,128)S(1)} %shard_map.105.full_in, f32[616,128]{1,0:T(8,128)S(1)} %get-tuple-element.20.wet_ref, ...), custom_call_target="tpu_custom_call" | custom-call | flops 20000000000 | bytes 1000 | tf_op jit(solution)/shard_map/pallas_call | solution.py:466
Async XLA Ops:
  5.3 8.2 %collective-permute-start = (f32[10,8,128]{2,1,0:T(8,128)S(1)}, f32[10,8,128]{2,1,0:T(8,128)S(1)}, u32[]{:S(2)}, u32[]{:S(2)}) collective-permute-start(f32[10,8,128]{2,1,0:T(8,128)S(1)} %get-tuple-element.17.on_own), channel_id=1, source_target_pairs={{0,16},{1,17},{2,18},{3,19},{4,20},{5,21},{6,22},{7,23},{8,24},{9,... | collective-permute-start | bytes 122888 | tf_op jit(solution)/shard_map/ppermute | solution.py:513
  5.4 8.2 %collective-permute-start.1 = (f32[10,8,128]{2,1,0:T(8,128)S(1)}, f32[10,8,128]{2,1,0:T(8,128)S(1)}, u32[]{:S(2)}, u32[]{:S(2)}) collective-permute-start(f32[10,8,128]{2,1,0:T(8,128)S(1)} %get-tuple-element.18.off_own), channel_id=1, source_target_pairs={{0,240},{1,241},{2,242},{3,243},{4,244},{5,245},{6,246},{7,247},{8... | collective-permute-start | bytes 122888 | tf_op jit(solution)/shard_map/ppermute | solution.py:514
  10.8 11.0 %collective-permute-start.4 = (f32[344,128]{1,0:T(8,128)S(1)}, f32[344,128]{1,0:T(8,128)S(1)}, u32[]{:S(2)}, u32[]{:S(2)}) collective-permute-start(f32[344,128]{1,0:T(8,128)S(1)} %get-tuple-element.25), channel_id=1, source_target_pairs={{15,254},{31,238},{47,222},{63,206},{79,190},{95,174},{111,158},{1... | collective-permute-start | bytes 528392 | tf_op jit(solution)/shard_map/ppermute | solution.py:521
  12.1 16.5 %collective-permute-start.2 = (f32[680,128]{1,0:T(8,128)S(1)}, f32[680,128]{1,0:T(8,128)S(1)}, u32[]{:S(2)}, u32[]{:S(2)}) collective-permute-start(f32[680,128]{1,0:T(8,128)S(1)} %get-tuple-element.21.xs_own), channel_id=1, source_target_pairs={{0,1},{1,0},{2,3},{3,2},{4,5},{5,4},{6,7},{7,6},{8,9},{9,8},{10,11... | collective-permute-start | bytes 1044488 | tf_op jit(solution)/shard_map/ppermute | solution.py:522
  14.3 14.3 %collective-permute-start.8 = (f32[24,128]{1,0:T(8,128)S(1)}, f32[24,128]{1,0:T(8,128)S(1)}, u32[]{:S(2)}, u32[]{:S(2)}) collective-permute-start(f32[24,128]{1,0:T(8,128)S(1)} %get-tuple-element.27), channel_id=1, source_target_pairs={{0,1},{1,0},{2,3},{3,2},{4,5},{5,4},{6,7},{7,6},{8,9},{9,8},{10,11... | collective-permute-start | bytes 36872 | tf_op jit(solution)/shard_map/ppermute | solution.py:531
  15.0 9.3 %collective-permute-start.6 = (f32[360,128]{1,0:T(8,128)S(1)}, f32[360,128]{1,0:T(8,128)S(1)}, u32[]{:S(2)}, u32[]{:S(2)}) collective-permute-start(f32[360,128]{1,0:T(8,128)S(1)} %get-tuple-element.26), channel_id=1, source_target_pairs={{15,254},{31,238},{47,222},{63,206},{79,190},{95,174},{111,158},{1... | collective-permute-start | bytes 552968 | tf_op jit(solution)/shard_map/ppermute | solution.py:529
  21.1 8.1 %collective-permute-start.3 = (f32[704,128]{1,0:T(8,128)S(1)}, f32[704,128]{1,0:T(8,128)S(1)}, u32[]{:S(2)}, u32[]{:S(2)}) collective-permute-start(f32[704,128]{1,0:T(8,128)S(1)} %get-tuple-element.24.zb_own), channel_id=1, source_target_pairs={{1,2},{2,1},{3,4},{4,3},{5,6},{6,5},{7,8},{8,7},{9,10},{10,9},{11,... | collective-permute-start | bytes 1081352 | tf_op jit(solution)/shard_map/ppermute | solution.py:530
  21.8 7.4 %collective-permute-start.5 = (f32[344,128]{1,0:T(8,128)S(1)}, f32[344,128]{1,0:T(8,128)S(1)}, u32[]{:S(2)}, u32[]{:S(2)}) collective-permute-start(f32[344,128]{1,0:T(8,128)S(1)} %collective-permute-done.4), channel_id=1, source_target_pairs={{14,15},{30,31},{46,47},{62,63},{78,79},{94,95},{110,111},{126,127... | collective-permute-start | bytes 528392 | tf_op jit(solution)/shard_map/ppermute | solution.py:532
  24.3 8.8 %collective-permute-start.7 = (f32[360,128]{1,0:T(8,128)S(1)}, f32[360,128]{1,0:T(8,128)S(1)}, u32[]{:S(2)}, u32[]{:S(2)}) collective-permute-start(f32[360,128]{1,0:T(8,128)S(1)} %collective-permute-done.6), channel_id=1, source_target_pairs={{14,15},{30,31},{46,47},{62,63},{78,79},{94,95},{110,111},{126,127... | collective-permute-start | bytes 552968 | tf_op jit(solution)/shard_map/ppermute | solution.py:533

commit v5 on v4

--- a/solution.py
+++ b/solution.py
@@ -19,7 +19,7 @@
 UNROLL_B = 25
 UNROLL_C = 16
 UNROLL_D = 25
-PART = 344
+PART = 448
 W_ROWS = 2*10**10
 W_CORNER = 2*10**10
 W_ADD = 2*10**10
@@ -245,10 +245,11 @@
     @pl.when(place[1] == tops)
     def _():
         rows = pl.ds(8 + 7, levels, stride=8)
-        planes = [state[i, rows, :] for i in range(4)] + [wet_ref[rows, :]]
+        planes = [state[i, rows, :] for i in range(4)] + [wet_ref[rows, :]] + [part[i, rows, :] for i in range(4)]
         for i, plane in enumerate(planes):
             count = min(levels, PART - levels * i)
-            fold_a[pl.ds(levels * i, count), :] = plane[:count]
+            if count > 0:
+                fold_a[pl.ds(levels * i, count), :] = plane[:count]
 
 
 def sides_of(lon_odd, on_own, off_own, on, off):

time: 37.8 us -> 37.5 us (level)
  the two profiles are of different devices: /device:TPU:226 before, /device:TPU:250 now
where the time goes in v5:
time: 37.5 us; the launch traced here: 37.2 us
  starting transfers between devices  15 us (40%)
  Pallas kernels  11.9 us (32%)
  waiting for transfers between devices  9.58 us (26%)
  between operations  0.73 us (2%)
    pallas_call x6, Pallas kernels, call(): pl.pallas_call(kernel, out_shape=outs, in_specs=[pl.BlockSpec(memory_spac...  11.9 us
    ppermute x1, starting transfers between devices, per_device(): fold_b = move(fold_b, perm=to_relay)  5.45 us
    ppermute x1, waiting for transfers between devices, per_device(): fold_a = move(fold_a, perm=from_relay)  3.77 us
    ppermute x1, waiting for transfers between devices, per_device(): corner_xs = move(corner_xs, perm=xs_pairs)  3.29 us
    ppermute x1, starting transfers between devices, per_device(): off = move(off_own, perm=off_pairs)  2.41 us
    ppermute x1, waiting for transfers between devices, per_device(): fold_b = move(fold_b, perm=from_relay)  1.97 us
    ppermute x1, starting transfers between devices, per_device(): fold_a = move(fold_a, perm=to_relay)  1.94 us
    ppermute x1, starting transfers between devices, per_device(): fold_a = move(fold_a, perm=from_relay)  1.29 us
  transfers between devices with their start and end apart: 9, of which 5 were waited for; matrix products, arithmetic and copies ran while one was open for 0% of the time, Pallas kernels for 8%

profile of v5, /device:TPU:250, one launch (start us, length us, event | category | flops | bytes accessed | tf_op | source)
XLA Modules:
  0.0 37.2 jit_solution(7098821483591124911)
XLA Ops:
  0.6 0.1 pad_add_fusion.place
  0.7 4.6 %shard_map.102 = (f32[4,616,128]{2,1,0:T(8,128)S(1)}, f32[616,128]{1,0:T(8,128)S(1)}, f32[10,8,128]{2,1,0:T(8,128)S(1)}, f32[10,8,128]{2,1,0:T(8,128)S(1)}, f32[...) custom-call(s32[2]{0:T(128)S(1)} %pad_add_fusion.place, f32[75,8,128]{2,1,0:T(8,128)} %temp_hbm.1, ...), custom_call_target="tpu_custom_call" | custom-call | flops 20000000000 | bytes 1000 | tf_op jit(solution)/shard_map/pallas_call | solution.py:467
  5.3 0.1 collective-permute-start
  5.4 2.4 %collective-permute-start.1 = (f32[10,8,128]{2,1,0:T(8,128)S(1)}, f32[10,8,128]{2,1,0:T(8,128)S(1)}, u32[]{:S(2)}, u32[]{:S(2)}) collective-permute-start(f32[10,8,128]{2,1,0:T(8,128)S(1)} %get-tuple-element.18.off_own), channel_id=1, source_target_pairs={{0,240},{1,241},{2,242},{3,243},{4,244},{5,245},{6,246},{7,247},{8... | collective-permute-start | bytes 122888 | tf_op jit(solution)/shard_map/ppermute | solution.py:515
  7.8 0.7 %shard_map.103 = (f32[680,128]{1,0:T(8,128)S(1)}, f32[448,128]{1,0:T(8,128)S(1)}) custom-call(s32[2]{0:T(128)S(1)} %pad_add_fusion.place, f32[4,616,128]{2,1,0:T(8,128)S(1)} %get-tuple-element.19.state, f32[616,128]{1,0:T(8,128)S(1)} %get-tuple-element.20.wet_ref, f32[4,616,128]{2,1,0:T(8,128)S(1)} %get-tuple-element.16.part), custom_call_target="tpu_custom_call" | custom-call | flops 20000000000 | bytes 1000 | tf_op jit(solution)/shard_map/pallas_call | solution.py:467
  8.5 1.9 %collective-permute-start.4 = (f32[448,128]{1,0:T(8,128)S(1)}, f32[448,128]{1,0:T(8,128)S(1)}, u32[]{:S(2)}, u32[]{:S(2)}) collective-permute-start(f32[448,128]{1,0:T(8,128)S(1)} %get-tuple-element.25), channel_id=1, source_target_pairs={{15,254},{31,238},{47,222},{63,206},{79,190},{95,174},{111,158},{1... | collective-permute-start | bytes 688136 | tf_op jit(solution)/shard_map/ppermute | solution.py:522
  10.5 0.8 %collective-permute-start.2 = (f32[680,128]{1,0:T(8,128)S(1)}, f32[680,128]{1,0:T(8,128)S(1)}, u32[]{:S(2)}, u32[]{:S(2)}) collective-permute-start(f32[680,128]{1,0:T(8,128)S(1)} %get-tuple-element.21.xs_own), channel_id=1, source_target_pairs={{0,1},{1,0},{2,3},{3,2},{4,5},{5,4},{6,7},{7,6},{8,9},{9,8},{10,11... | collective-permute-start | bytes 1044488 | tf_op jit(solution)/shard_map/ppermute | solution.py:523
  11.3 0.0 collective-permute-done.on
  11.3 0.3 collective-permute-done.1.off
  11.7 0.7 %shard_map.104 = (f32[704,128]{1,0:T(8,128)S(1)}, f32[256,128]{1,0:T(8,128)S(1)}, f32[24,128]{1,0:T(8,128)S(1)}, f32[8,8,128]{2,1,0:T(8,128)S(1)}) custom-call(s32[2]{0:T(128)S(1)} %pad_add_fusion.place, f32[10,8,128]{2,1,0:T(8,128)S(1)} %get-tuple-element.17.on_own, f32[10,8,128]{2,1,0:T(8,128)S(1)} %get-tuple-element.18.off_own, ...), custom_call_target="tpu_custom_call" | custom-call | flops 20000000000 | bytes 1000 | tf_op jit(solution)/shard_map/pallas_call | solution.py:467
  12.4 1.0 %collective-permute-start.8 = (f32[24,128]{1,0:T(8,128)S(1)}, f32[24,128]{1,0:T(8,128)S(1)}, u32[]{:S(2)}, u32[]{:S(2)}) collective-permute-start(f32[24,128]{1,0:T(8,128)S(1)} %get-tuple-element.27), channel_id=1, source_target_pairs={{0,1},{1,0},{2,3},{3,2},{4,5},{5,4},{6,7},{7,6},{8,9},{9,8},{10,11... | collective-permute-start | bytes 36872 | tf_op jit(solution)/shard_map/ppermute | solution.py:532
  13.4 5.4 %collective-permute-start.6 = (f32[256,128]{1,0:T(8,128)S(1)}, f32[256,128]{1,0:T(8,128)S(1)}, u32[]{:S(2)}, u32[]{:S(2)}) collective-permute-start(f32[256,128]{1,0:T(8,128)S(1)} %get-tuple-element.26), channel_id=1, source_target_pairs={{15,254},{31,238},{47,222},{63,206},{79,190},{95,174},{111,158},{1... | collective-permute-start | bytes 393224 | tf_op jit(solution)/shard_map/ppermute | solution.py:530
  18.8 0.7 %collective-permute-start.3 = (f32[704,128]{1,0:T(8,128)S(1)}, f32[704,128]{1,0:T(8,128)S(1)}, u32[]{:S(2)}, u32[]{:S(2)}) collective-permute-start(f32[704,128]{1,0:T(8,128)S(1)} %get-tuple-element.24.zb_own), channel_id=1, source_target_pairs={{1,2},{2,1},{3,4},{4,3},{5,6},{6,5},{7,8},{8,7},{9,10},{10,9},{11,... | collective-permute-start | bytes 1081352 | tf_op jit(solution)/shard_map/ppermute | solution.py:531
  19.5 0.0 collective-permute-done.4
  19.5 1.3 %collective-permute-start.5 = (f32[448,128]{1,0:T(8,128)S(1)}, f32[448,128]{1,0:T(8,128)S(1)}, u32[]{:S(2)}, u32[]{:S(2)}) collective-permute-start(f32[448,128]{1,0:T(8,128)S(1)} %collective-permute-done.4), channel_id=1, source_target_pairs={{14,15},{30,31},{46,47},{62,63},{78,79},{94,95},{110,111},{126,127... | collective-permute-start | bytes 688136 | tf_op jit(solution)/shard_map/ppermute | solution.py:533
  20.8 1.2 %shard_map.105.full_in = f32[4,616,128]{2,1,0:T(8,128)S(1)} custom-call(s32[2]{0:T(128)S(1)} %pad_add_fusion.place, f32[4,616,128]{2,1,0:T(8,128)S(1)} %get-tuple-element.16.part, f32[8,8,128]{2,1,0:T(8,128)S(1)} %get-tuple-element.22.extra), custom_call_target="tpu_custom_call" | custom-call | flops 20000000000 | bytes 1000 | tf_op jit(solution)/shard_map/pallas_call | solution.py:467
  22.0 0.2 collective-permute-done.6
  22.2 1.3 %collective-permute-start.7 = (f32[256,128]{1,0:T(8,128)S(1)}, f32[256,128]{1,0:T(8,128)S(1)}, u32[]{:S(2)}, u32[]{:S(2)}) collective-permute-start(f32[256,128]{1,0:T(8,128)S(1)} %collective-permute-done.6), channel_id=1, source_target_pairs={{14,15},{30,31},{46,47},{62,63},{78,79},{94,95},{110,111},{126,127... | collective-permute-start | bytes 393224 | tf_op jit(solution)/shard_map/ppermute | solution.py:534
  23.5 3.3 %collective-permute-done.8.corner_xs = f32[24,128]{1,0:T(8,128)S(1)} collective-permute-done((f32[24,128]{1,0:T(8,128)S(1)}, f32[24,128]{1,0:T(8,128)S(1)}, u32[]{:S(2)}, u32[]{:S(2)}) %collective-permute-start.8) | collective-permute-done | bytes 12320 | tf_op jit(solution)/shard_map/ppermute | solution.py:532
  26.8 0.0 collective-permute-done.2.refs_0_.xs
  26.8 0.0 collective-permute-done.3.zb
  26.8 3.8 %collective-permute-done.5.refs_1_.fold_a = f32[448,128]{1,0:T(8,128)S(1)} collective-permute-done((f32[448,128]{1,0:T(8,128)S(1)}, f32[448,128]{1,0:T(8,128)S(1)}, u32[]{:S(2)}, u32[]{:S(2)}) %collective-permute-start.5) | collective-permute-done | bytes 229408 | tf_op jit(solution)/shard_map/ppermute | solution.py:533
  30.6 0.6 %shard_map.106.corners = f32[48,128]{1,0:T(8,128)S(1)} custom-call(s32[2]{0:T(128)S(1)} %pad_add_fusion.place, f32[704,128]{1,0:T(8,128)S(1)} %collective-permute-done.3.zb, f32[24,128]{1,0:T(8,128)S(1)} %collective-permute-done.8.corner_xs, f32[680,128]{1,0:T(8,128)S(1)} %collective-permute-done.2.refs_0_.xs, ...), custom_call_target="tpu_custom_call" | custom-call | flops 20000000000 | bytes 1000 | tf_op jit(solution)/shard_map/pallas_call | solution.py:467
  31.1 2.0 %collective-permute-done.7.fold_b = f32[256,128]{1,0:T(8,128)S(1)} collective-permute-done((f32[256,128]{1,0:T(8,128)S(1)}, f32[256,128]{1,0:T(8,128)S(1)}, u32[]{:S(2)}, u32[]{:S(2)}) %collective-permute-start.7) | collective-permute-done | bytes 131104 | tf_op jit(solution)/shard_map/ppermute | solution.py:534
  33.1 4.2 %shard_map.107 = (f32[75,8,128]{2,1,0:T(8,128)}, f32[75,8,128]{2,1,0:T(8,128)}, f32[75,8,128]{2,1,0:T(8,128)}, f32[75,8,128]{2,1,0:T(8,128)}) custom-call(s32[2]{0:T(128)S(1)} %pad_add_fusion.place, f32[4,616,128]{2,1,0:T(8,128)S(1)} %shard_map.105.full_in, f32[616,128]{1,0:T(8,128)S(1)} %get-tuple-element.20.wet_ref, ...), custom_call_target="tpu_custom_call" | custom-call | flops 20000000000 | bytes 1000 | tf_op jit(solution)/shard_map/pallas_call | solution.py:467
Async XLA Ops:
  5.3 6.0 %collective-permute-start = (f32[10,8,128]{2,1,0:T(8,128)S(1)}, f32[10,8,128]{2,1,0:T(8,128)S(1)}, u32[]{:S(2)}, u32[]{:S(2)}) collective-permute-start(f32[10,8,128]{2,1,0:T(8,128)S(1)} %get-tuple-element.17.on_own), channel_id=1, source_target_pairs={{0,16},{1,17},{2,18},{3,19},{4,20},{5,21},{6,22},{7,23},{8,24},{9,... | collective-permute-start | bytes 122888 | tf_op jit(solution)/shard_map/ppermute | solution.py:514
  5.4 6.2 %collective-permute-start.1 = (f32[10,8,128]{2,1,0:T(8,128)S(1)}, f32[10,8,128]{2,1,0:T(8,128)S(1)}, u32[]{:S(2)}, u32[]{:S(2)}) collective-permute-start(f32[10,8,128]{2,1,0:T(8,128)S(1)} %get-tuple-element.18.off_own), channel_id=1, source_target_pairs={{0,240},{1,241},{2,242},{3,243},{4,244},{5,245},{6,246},{7,247},{8... | collective-permute-start | bytes 122888 | tf_op jit(solution)/shard_map/ppermute | solution.py:515
  8.5 11.0 %collective-permute-start.4 = (f32[448,128]{1,0:T(8,128)S(1)}, f32[448,128]{1,0:T(8,128)S(1)}, u32[]{:S(2)}, u32[]{:S(2)}) collective-permute-start(f32[448,128]{1,0:T(8,128)S(1)} %get-tuple-element.25), channel_id=1, source_target_pairs={{15,254},{31,238},{47,222},{63,206},{79,190},{95,174},{111,158},{1... | collective-permute-start | bytes 688136 | tf_op jit(solution)/shard_map/ppermute | solution.py:522
  10.5 16.3 %collective-permute-start.2 = (f32[680,128]{1,0:T(8,128)S(1)}, f32[680,128]{1,0:T(8,128)S(1)}, u32[]{:S(2)}, u32[]{:S(2)}) collective-permute-start(f32[680,128]{1,0:T(8,128)S(1)} %get-tuple-element.21.xs_own), channel_id=1, source_target_pairs={{0,1},{1,0},{2,3},{3,2},{4,5},{5,4},{6,7},{7,6},{8,9},{9,8},{10,11... | collective-permute-start | bytes 1044488 | tf_op jit(solution)/shard_map/ppermute | solution.py:523
  12.4 14.4 %collective-permute-start.8 = (f32[24,128]{1,0:T(8,128)S(1)}, f32[24,128]{1,0:T(8,128)S(1)}, u32[]{:S(2)}, u32[]{:S(2)}) collective-permute-start(f32[24,128]{1,0:T(8,128)S(1)} %get-tuple-element.27), channel_id=1, source_target_pairs={{0,1},{1,0},{2,3},{3,2},{4,5},{5,4},{6,7},{7,6},{8,9},{9,8},{10,11... | collective-permute-start | bytes 36872 | tf_op jit(solution)/shard_map/ppermute | solution.py:532
  13.4 8.8 %collective-permute-start.6 = (f32[256,128]{1,0:T(8,128)S(1)}, f32[256,128]{1,0:T(8,128)S(1)}, u32[]{:S(2)}, u32[]{:S(2)}) collective-permute-start(f32[256,128]{1,0:T(8,128)S(1)} %get-tuple-element.26), channel_id=1, source_target_pairs={{15,254},{31,238},{47,222},{63,206},{79,190},{95,174},{111,158},{1... | collective-permute-start | bytes 393224 | tf_op jit(solution)/shard_map/ppermute | solution.py:530
  18.8 8.0 %collective-permute-start.3 = (f32[704,128]{1,0:T(8,128)S(1)}, f32[704,128]{1,0:T(8,128)S(1)}, u32[]{:S(2)}, u32[]{:S(2)}) collective-permute-start(f32[704,128]{1,0:T(8,128)S(1)} %get-tuple-element.24.zb_own), channel_id=1, source_target_pairs={{1,2},{2,1},{3,4},{4,3},{5,6},{6,5},{7,8},{8,7},{9,10},{10,9},{11,... | collective-permute-start | bytes 1081352 | tf_op jit(solution)/shard_map/ppermute | solution.py:531
  19.5 11.0 %collective-permute-start.5 = (f32[448,128]{1,0:T(8,128)S(1)}, f32[448,128]{1,0:T(8,128)S(1)}, u32[]{:S(2)}, u32[]{:S(2)}) collective-permute-start(f32[448,128]{1,0:T(8,128)S(1)} %collective-permute-done.4), channel_id=1, source_target_pairs={{14,15},{30,31},{46,47},{62,63},{78,79},{94,95},{110,111},{126,127... | collective-permute-start | bytes 688136 | tf_op jit(solution)/shard_map/ppermute | solution.py:533
  22.2 10.9 %collective-permute-start.7 = (f32[256,128]{1,0:T(8,128)S(1)}, f32[256,128]{1,0:T(8,128)S(1)}, u32[]{:S(2)}, u32[]{:S(2)}) collective-permute-start(f32[256,128]{1,0:T(8,128)S(1)} %collective-permute-done.6), channel_id=1, source_target_pairs={{14,15},{30,31},{46,47},{62,63},{78,79},{94,95},{110,111},{126,127... | collective-permute-start | bytes 393224 | tf_op jit(solution)/shard_map/ppermute | solution.py:534

commit v6 on v5

--- a/solution.py
+++ b/solution.py
@@ -485,8 +485,8 @@
     xs = [(at(o, a), at(o, a ^ 1)) for o, a in every]
     zb = [(at(o, a), at(o, a + 1 if a % 2 else a - 1)) for o, a in every if 0 < a < count_lat - 1]
     top = count_lat - 1
-    to_relay = [(at(o, top), at(count_lon - 1 - o, top - 1)) for o in range(count_lon)]
-    from_relay = [(at(o, top - 1), at(o, top)) for o in range(count_lon)]
+    to_relay = [(at(o, top), at(o ^ 3, top - 1)) for o in range(count_lon)]
+    from_relay = [(at(o ^ 3, top - 1), at(count_lon - 1 - o, top)) for o in range(count_lon)]
     return on, off, xs, zb, to_relay, from_relay
 
 

time: 37.5 us -> 37.8 us (level)
  the two profiles are of different devices: /device:TPU:250 before, /device:TPU:226 now
where the time goes in v6:
time: 37.8 us; the launch traced here: 37.6 us
  starting transfers between devices  15.5 us (41%)
  Pallas kernels  11.9 us (31%)
  waiting for transfers between devices  9.39 us (25%)
  between operations  0.74 us (2%)
    pallas_call x6, Pallas kernels, call(): pl.pallas_call(kernel, out_shape=outs, in_specs=[pl.BlockSpec(memory_spac...  11.9 us
    ppermute x1, waiting for transfers between devices, per_device(): fold_a = move(fold_a, perm=from_relay)  4.94 us
    ppermute x1, starting transfers between devices, per_device(): off = move(off_own, perm=off_pairs)  4.68 us
    ppermute x1, starting transfers between devices, per_device(): fold_b = move(fold_b, perm=to_relay)  3.97 us
    ppermute x1, waiting for transfers between devices, per_device(): corner_xs = move(corner_xs, perm=xs_pairs)  3.59 us
    ppermute x1, starting transfers between devices, per_device(): xs = move(xs_own, perm=xs_pairs)  1.46 us
    ppermute x1, starting transfers between devices, per_device(): fold_a = move(fold_a, perm=to_relay)  1.3 us
    ppermute x1, starting transfers between devices, per_device(): fold_a = move(fold_a, perm=from_relay)  1.29 us
  transfers between devices with their start and end apart: 9, of which 3 were waited for; matrix products, arithmetic and copies ran while one was open for 0% of the time, Pallas kernels for 8%

profile of v6, /device:TPU:226, one launch (start us, length us, event | category | flops | bytes accessed | tf_op | source)
XLA Modules:
  0.0 37.6 jit_solution(6319223735613530643)
XLA Ops:
  0.6 0.1 pad_add_fusion.place
  0.7 4.6 %shard_map.102 = (f32[4,616,128]{2,1,0:T(8,128)S(1)}, f32[616,128]{1,0:T(8,128)S(1)}, f32[10,8,128]{2,1,0:T(8,128)S(1)}, f32[10,8,128]{2,1,0:T(8,128)S(1)}, f32[...) custom-call(s32[2]{0:T(128)S(1)} %pad_add_fusion.place, f32[75,8,128]{2,1,0:T(8,128)} %temp_hbm.1, ...), custom_call_target="tpu_custom_call" | custom-call | flops 20000000000 | bytes 1000 | tf_op jit(solution)/shard_map/pallas_call | solution.py:467
  5.3 0.1 collective-permute-start
  5.4 4.7 %collective-permute-start.1 = (f32[10,8,128]{2,1,0:T(8,128)S(1)}, f32[10,8,128]{2,1,0:T(8,128)S(1)}, u32[]{:S(2)}, u32[]{:S(2)}) collective-permute-start(f32[10,8,128]{2,1,0:T(8,128)S(1)} %get-tuple-element.18.off_own), channel_id=1, source_target_pairs={{0,240},{1,241},{2,242},{3,243},{4,244},{5,245},{6,246},{7,247},{8... | collective-permute-start | bytes 122888 | tf_op jit(solution)/shard_map/ppermute | solution.py:515
  10.1 0.7 %shard_map.103 = (f32[680,128]{1,0:T(8,128)S(1)}, f32[448,128]{1,0:T(8,128)S(1)}) custom-call(s32[2]{0:T(128)S(1)} %pad_add_fusion.place, f32[4,616,128]{2,1,0:T(8,128)S(1)} %get-tuple-element.19.state, f32[616,128]{1,0:T(8,128)S(1)} %get-tuple-element.20.wet_ref, f32[4,616,128]{2,1,0:T(8,128)S(1)} %get-tuple-element.16.part), custom_call_target="tpu_custom_call" | custom-call | flops 20000000000 | bytes 1000 | tf_op jit(solution)/shard_map/pallas_call | solution.py:467
  10.8 1.3 %collective-permute-start.4 = (f32[448,128]{1,0:T(8,128)S(1)}, f32[448,128]{1,0:T(8,128)S(1)}, u32[]{:S(2)}, u32[]{:S(2)}) collective-permute-start(f32[448,128]{1,0:T(8,128)S(1)} %get-tuple-element.25), channel_id=1, source_target_pairs={{15,62},{31,46},{47,30},{63,14},{79,126},{95,110},{111,94},{127,78... | collective-permute-start | bytes 688136 | tf_op jit(solution)/shard_map/ppermute | solution.py:522
  12.1 1.5 %collective-permute-start.2 = (f32[680,128]{1,0:T(8,128)S(1)}, f32[680,128]{1,0:T(8,128)S(1)}, u32[]{:S(2)}, u32[]{:S(2)}) collective-permute-start(f32[680,128]{1,0:T(8,128)S(1)} %get-tuple-element.21.xs_own), channel_id=1, source_target_pairs={{0,1},{1,0},{2,3},{3,2},{4,5},{5,4},{6,7},{7,6},{8,9},{9,8},{10,11... | collective-permute-start | bytes 1044488 | tf_op jit(solution)/shard_map/ppermute | solution.py:523
  13.6 0.0 collective-permute-done.on
  13.6 0.0 collective-permute-done.1.off
  13.6 0.7 %shard_map.104 = (f32[704,128]{1,0:T(8,128)S(1)}, f32[256,128]{1,0:T(8,128)S(1)}, f32[24,128]{1,0:T(8,128)S(1)}, f32[8,8,128]{2,1,0:T(8,128)S(1)}) custom-call(s32[2]{0:T(128)S(1)} %pad_add_fusion.place, f32[10,8,128]{2,1,0:T(8,128)S(1)} %get-tuple-element.17.on_own, f32[10,8,128]{2,1,0:T(8,128)S(1)} %get-tuple-element.18.off_own, ...), custom_call_target="tpu_custom_call" | custom-call | flops 20000000000 | bytes 1000 | tf_op jit(solution)/shard_map/pallas_call | solution.py:467
  14.3 0.7 %collective-permute-start.8 = (f32[24,128]{1,0:T(8,128)S(1)}, f32[24,128]{1,0:T(8,128)S(1)}, u32[]{:S(2)}, u32[]{:S(2)}) collective-permute-start(f32[24,128]{1,0:T(8,128)S(1)} %get-tuple-element.27), channel_id=1, source_target_pairs={{0,1},{1,0},{2,3},{3,2},{4,5},{5,4},{6,7},{7,6},{8,9},{9,8},{10,11... | collective-permute-start | bytes 36872 | tf_op jit(solution)/shard_map/ppermute | solution.py:532
  15.0 4.0 %collective-permute-start.6 = (f32[256,128]{1,0:T(8,128)S(1)}, f32[256,128]{1,0:T(8,128)S(1)}, u32[]{:S(2)}, u32[]{:S(2)}) collective-permute-start(f32[256,128]{1,0:T(8,128)S(1)} %get-tuple-element.26), channel_id=1, source_target_pairs={{15,62},{31,46},{47,30},{63,14},{79,126},{95,110},{111,94},{127,78... | collective-permute-start | bytes 393224 | tf_op jit(solution)/shard_map/ppermute | solution.py:530
  19.0 0.7 %collective-permute-start.3 = (f32[704,128]{1,0:T(8,128)S(1)}, f32[704,128]{1,0:T(8,128)S(1)}, u32[]{:S(2)}, u32[]{:S(2)}) collective-permute-start(f32[704,128]{1,0:T(8,128)S(1)} %get-tuple-element.24.zb_own), channel_id=1, source_target_pairs={{1,2},{2,1},{3,4},{4,3},{5,6},{6,5},{7,8},{8,7},{9,10},{10,9},{11,... | collective-permute-start | bytes 1081352 | tf_op jit(solution)/shard_map/ppermute | solution.py:531
  19.7 0.0 collective-permute-done.4
  19.7 1.3 %collective-permute-start.5 = (f32[448,128]{1,0:T(8,128)S(1)}, f32[448,128]{1,0:T(8,128)S(1)}, u32[]{:S(2)}, u32[]{:S(2)}) collective-permute-start(f32[448,128]{1,0:T(8,128)S(1)} %collective-permute-done.4), channel_id=1, source_target_pairs={{62,255},{46,239},{30,223},{14,207},{126,191},{110,175},{94,159},{... | collective-permute-start | bytes 688136 | tf_op jit(solution)/shard_map/ppermute | solution.py:533
  21.0 1.2 %shard_map.105.full_in = f32[4,616,128]{2,1,0:T(8,128)S(1)} custom-call(s32[2]{0:T(128)S(1)} %pad_add_fusion.place, f32[4,616,128]{2,1,0:T(8,128)S(1)} %get-tuple-element.16.part, f32[8,8,128]{2,1,0:T(8,128)S(1)} %get-tuple-element.22.extra), custom_call_target="tpu_custom_call" | custom-call | flops 20000000000 | bytes 1000 | tf_op jit(solution)/shard_map/pallas_call | solution.py:467
  22.2 0.0 collective-permute-done.6
  22.2 1.3 %collective-permute-start.7 = (f32[256,128]{1,0:T(8,128)S(1)}, f32[256,128]{1,0:T(8,128)S(1)}, u32[]{:S(2)}, u32[]{:S(2)}) collective-permute-start(f32[256,128]{1,0:T(8,128)S(1)} %collective-permute-done.6), channel_id=1, source_target_pairs={{62,255},{46,239},{30,223},{14,207},{126,191},{110,175},{94,159},{... | collective-permute-start | bytes 393224 | tf_op jit(solution)/shard_map/ppermute | solution.py:534
  23.5 3.6 %collective-permute-done.8.corner_xs = f32[24,128]{1,0:T(8,128)S(1)} collective-permute-done((f32[24,128]{1,0:T(8,128)S(1)}, f32[24,128]{1,0:T(8,128)S(1)}, u32[]{:S(2)}, u32[]{:S(2)}) %collective-permute-start.8) | collective-permute-done | bytes 12320 | tf_op jit(solution)/shard_map/ppermute | solution.py:532
  27.1 0.0 collective-permute-done.2.refs_0_.xs
  27.1 0.0 collective-permute-done.3.zb
  27.1 4.9 %collective-permute-done.5.refs_1_.fold_a = f32[448,128]{1,0:T(8,128)S(1)} collective-permute-done((f32[448,128]{1,0:T(8,128)S(1)}, f32[448,128]{1,0:T(8,128)S(1)}, u32[]{:S(2)}, u32[]{:S(2)}) %collective-permute-start.5) | collective-permute-done | bytes 229408 | tf_op jit(solution)/shard_map/ppermute | solution.py:533
  32.0 0.6 %shard_map.106.corners = f32[48,128]{1,0:T(8,128)S(1)} custom-call(s32[2]{0:T(128)S(1)} %pad_add_fusion.place, f32[704,128]{1,0:T(8,128)S(1)} %collective-permute-done.3.zb, f32[24,128]{1,0:T(8,128)S(1)} %collective-permute-done.8.corner_xs, f32[680,128]{1,0:T(8,128)S(1)} %collective-permute-done.2.refs_0_.xs, ...), custom_call_target="tpu_custom_call" | custom-call | flops 20000000000 | bytes 1000 | tf_op jit(solution)/shard_map/pallas_call | solution.py:467
  32.6 0.8 %collective-permute-done.7.fold_b = f32[256,128]{1,0:T(8,128)S(1)} collective-permute-done((f32[256,128]{1,0:T(8,128)S(1)}, f32[256,128]{1,0:T(8,128)S(1)}, u32[]{:S(2)}, u32[]{:S(2)}) %collective-permute-start.7) | collective-permute-done | bytes 131104 | tf_op jit(solution)/shard_map/ppermute | solution.py:534
  33.4 4.2 %shard_map.107 = (f32[75,8,128]{2,1,0:T(8,128)}, f32[75,8,128]{2,1,0:T(8,128)}, f32[75,8,128]{2,1,0:T(8,128)}, f32[75,8,128]{2,1,0:T(8,128)}) custom-call(s32[2]{0:T(128)S(1)} %pad_add_fusion.place, f32[4,616,128]{2,1,0:T(8,128)S(1)} %shard_map.105.full_in, f32[616,128]{1,0:T(8,128)S(1)} %get-tuple-element.20.wet_ref, ...), custom_call_target="tpu_custom_call" | custom-call | flops 20000000000 | bytes 1000 | tf_op jit(solution)/shard_map/pallas_call | solution.py:467
Async XLA Ops:
  5.3 8.2 %collective-permute-start = (f32[10,8,128]{2,1,0:T(8,128)S(1)}, f32[10,8,128]{2,1,0:T(8,128)S(1)}, u32[]{:S(2)}, u32[]{:S(2)}) collective-permute-start(f32[10,8,128]{2,1,0:T(8,128)S(1)} %get-tuple-element.17.on_own), channel_id=1, source_target_pairs={{0,16},{1,17},{2,18},{3,19},{4,20},{5,21},{6,22},{7,23},{8,24},{9,... | collective-permute-start | bytes 122888 | tf_op jit(solution)/shard_map/ppermute | solution.py:514
  5.4 8.2 %collective-permute-start.1 = (f32[10,8,128]{2,1,0:T(8,128)S(1)}, f32[10,8,128]{2,1,0:T(8,128)S(1)}, u32[]{:S(2)}, u32[]{:S(2)}) collective-permute-start(f32[10,8,128]{2,1,0:T(8,128)S(1)} %get-tuple-element.18.off_own), channel_id=1, source_target_pairs={{0,240},{1,241},{2,242},{3,243},{4,244},{5,245},{6,246},{7,247},{8... | collective-permute-start | bytes 122888 | tf_op jit(solution)/shard_map/ppermute | solution.py:515
  10.8 8.9 %collective-permute-start.4 = (f32[448,128]{1,0:T(8,128)S(1)}, f32[448,128]{1,0:T(8,128)S(1)}, u32[]{:S(2)}, u32[]{:S(2)}) collective-permute-start(f32[448,128]{1,0:T(8,128)S(1)} %get-tuple-element.25), channel_id=1, source_target_pairs={{15,62},{31,46},{47,30},{63,14},{79,126},{95,110},{111,94},{127,78... | collective-permute-start | bytes 688136 | tf_op jit(solution)/shard_map/ppermute | solution.py:522
  12.1 15.0 %collective-permute-start.2 = (f32[680,128]{1,0:T(8,128)S(1)}, f32[680,128]{1,0:T(8,128)S(1)}, u32[]{:S(2)}, u32[]{:S(2)}) collective-permute-start(f32[680,128]{1,0:T(8,128)S(1)} %get-tuple-element.21.xs_own), channel_id=1, source_target_pairs={{0,1},{1,0},{2,3},{3,2},{4,5},{5,4},{6,7},{7,6},{8,9},{9,8},{10,11... | collective-permute-start | bytes 1044488 | tf_op jit(solution)/shard_map/ppermute | solution.py:523
  14.3 12.8 %collective-permute-start.8 = (f32[24,128]{1,0:T(8,128)S(1)}, f32[24,128]{1,0:T(8,128)S(1)}, u32[]{:S(2)}, u32[]{:S(2)}) collective-permute-start(f32[24,128]{1,0:T(8,128)S(1)} %get-tuple-element.27), channel_id=1, source_target_pairs={{0,1},{1,0},{2,3},{3,2},{4,5},{5,4},{6,7},{7,6},{8,9},{9,8},{10,11... | collective-permute-start | bytes 36872 | tf_op jit(solution)/shard_map/ppermute | solution.py:532
  15.0 7.2 %collective-permute-start.6 = (f32[256,128]{1,0:T(8,128)S(1)}, f32[256,128]{1,0:T(8,128)S(1)}, u32[]{:S(2)}, u32[]{:S(2)}) collective-permute-start(f32[256,128]{1,0:T(8,128)S(1)} %get-tuple-element.26), channel_id=1, source_target_pairs={{15,62},{31,46},{47,30},{63,14},{79,126},{95,110},{111,94},{127,78... | collective-permute-start | bytes 393224 | tf_op jit(solution)/shard_map/ppermute | solution.py:530
  19.0 8.1 %collective-permute-start.3 = (f32[704,128]{1,0:T(8,128)S(1)}, f32[704,128]{1,0:T(8,128)S(1)}, u32[]{:S(2)}, u32[]{:S(2)}) collective-permute-start(f32[704,128]{1,0:T(8,128)S(1)} %get-tuple-element.24.zb_own), channel_id=1, source_target_pairs={{1,2},{2,1},{3,4},{4,3},{5,6},{6,5},{7,8},{8,7},{9,10},{10,9},{11,... | collective-permute-start | bytes 1081352 | tf_op jit(solution)/shard_map/ppermute | solution.py:531
  19.7 12.3 %collective-permute-start.5 = (f32[448,128]{1,0:T(8,128)S(1)}, f32[448,128]{1,0:T(8,128)S(1)}, u32[]{:S(2)}, u32[]{:S(2)}) collective-permute-start(f32[448,128]{1,0:T(8,128)S(1)} %collective-permute-done.4), channel_id=1, source_target_pairs={{62,255},{46,239},{30,223},{14,207},{126,191},{110,175},{94,159},{... | collective-permute-start | bytes 688136 | tf_op jit(solution)/shard_map/ppermute | solution.py:533
  22.2 11.2 %collective-permute-start.7 = (f32[256,128]{1,0:T(8,128)S(1)}, f32[256,128]{1,0:T(8,128)S(1)}, u32[]{:S(2)}, u32[]{:S(2)}) collective-permute-start(f32[256,128]{1,0:T(8,128)S(1)} %collective-permute-done.6), channel_id=1, source_target_pairs={{62,255},{46,239},{30,223},{14,207},{126,191},{110,175},{94,159},{... | collective-permute-start | bytes 393224 | tf_op jit(solution)/shard_map/ppermute | solution.py:534
